TPU v7x, 32 devices: a whole 2x2x4 slice. The times are simulated.
32 devices in a mesh: dop: 8 (over z, x), rng: 4 (over y, core).
Axes of the slice: x: 2, y: 2, z: 4, core: 2. Of those that a mesh axis runs over, the one named last changes fastest.
Arguments:
- raw_samples: bfloat16 [256, 96, 2, 4096], P('dop', 'rng'), may hold values from -16 to 16
- filter_taps: float32 [8, 512], replicated, may hold values from -2 to 2
- range_code: float32 [2, 7], replicated, may hold values from -1.6 to 1.6
- train_mask: int32 [16, 96], P('dop', 'rng'), may hold values 0 or 1
- steer_index: int32 [16, 4], P('dop'), may hold values from 0 to 255
Outputs:
- beam_out: float32 [2, 16, 4, 96], P(None, 'dop', None, 'rng')
All inputs are finite; a program needn't handle non-finite values. No bound on the sum of `train_mask` on one device may be relied on, other than what follows from the above.
Results may differ from a plain program's by a relative error of at most 0.012.
The roundings to bfloat16 on the way count: a program that leaves them out, or rounds other values in their place, can miss the bound.
Values may be sent and summed in bfloat16 or wider, within the bound.
A program may use at most 128 MiB of HBM per device.

v0:
```python
import math

import jax
import jax.numpy as jnp
from jax import lax
from jax.sharding import PartitionSpec as P

ELEMENTS = 256
CHANNELS = 512
TAPS = 8
CODE_REACH = 3


loading_level = 0.25


def padded_2(x, sides, width):
    for axis, dim in sides:
        count, length = (lax.axis_size(axis), x.shape[dim])
        up = [(i, (i + 1) % count) for i in range(count - 1)]
        down = [(j, i) for i, j in up]
        last = lax.slice_in_dim(x, length - width, length, axis=dim)
        leading = lax.slice_in_dim(x, 0, width, axis=dim)
        before = lax.ppermute(last, axis, up)
        after = lax.ppermute(leading, axis, down)
        x = jnp.concatenate([before, x, after], axis=dim)
    return x


def dft_table(bin_total):
    mode_index = jnp.arange(CHANNELS, dtype=jnp.int32)
    bin_index = jnp.arange(bin_total, dtype=jnp.int32)
    turn_count = jnp.mod(mode_index[:, None] * bin_index[None, :], CHANNELS).astype(jnp.float32)
    phases = turn_count * (2.0 * math.pi / CHANNELS)
    cosine = jnp.cos(phases) / math.sqrt(CHANNELS)
    sine_part = jnp.sin(phases) / math.sqrt(CHANNELS)
    top_half = jnp.concatenate([cosine, -sine_part], axis=1)
    low_half = jnp.concatenate([sine_part, cosine], axis=1)
    return jnp.concatenate([top_half, low_half], axis=0).astype(jnp.bfloat16)


def compress(padded, range_code):
    gate_count = padded.shape[1] - 2 * CODE_REACH
    shape_out = (padded.shape[0], gate_count, padded.shape[3])
    real_sum = jnp.zeros(shape_out, jnp.float32)
    imag_sum = jnp.zeros(shape_out, jnp.float32)
    for offset in range(2 * CODE_REACH + 1):
        window = lax.slice_in_dim(padded, offset, offset + gate_count, axis=1).astype(jnp.float32)
        real_sum = (
            real_sum
            + range_code[0, offset] * window[:, :, 0]
            - range_code[1, offset] * window[:, :, 1]
        )
        imag_sum = (
            imag_sum
            + range_code[0, offset] * window[:, :, 1]
            + range_code[1, offset] * window[:, :, 0]
        )
    return jnp.stack([real_sum, imag_sum], axis=2).astype(jnp.bfloat16)


def local_gram(masked):
    real_rows = masked[:, :, 0]
    imag_rows = masked[:, :, 1]
    top_rows = jnp.concatenate([real_rows, imag_rows], axis=2)
    low_rows = jnp.concatenate([-imag_rows, real_rows], axis=2)
    stacked = jnp.concatenate([top_rows, low_rows], axis=1)
    return jnp.einsum("bri,brj->bij", stacked, stacked, preferred_element_type=jnp.float32)


def steering_table(steer_rows):
    element = jnp.arange(ELEMENTS, dtype=jnp.int32)
    turn_count = jnp.mod(
        element[None, :, None] * (2 * steer_rows[:, None, :] - ELEMENTS), 2 * ELEMENTS
    ).astype(jnp.float32)
    phases = turn_count * (math.pi / ELEMENTS)
    return jnp.concatenate([jnp.cos(phases), jnp.sin(phases)], axis=1)


def solve_all(factor, steering):
    return jax.vmap(
        lambda lower_part, target: jax.scipy.linalg.cho_solve((lower_part, True), target)
    )(factor, steering)


def beam_output(compressed, weights, steering):
    response = jnp.sum(steering * weights, axis=1)
    signal = compressed.astype(jnp.float32)
    weight_real = weights[:, :ELEMENTS]
    weight_imag = weights[:, ELEMENTS:]
    highest = lax.Precision.HIGHEST
    out_real = jnp.einsum(
        "bik,bgi->bkg", weight_real, signal[:, :, 0], precision=highest
    ) + jnp.einsum("bik,bgi->bkg", weight_imag, signal[:, :, 1], precision=highest)
    out_imag = jnp.einsum(
        "bik,bgi->bkg", weight_real, signal[:, :, 1], precision=highest
    ) - jnp.einsum("bik,bgi->bkg", weight_imag, signal[:, :, 0], precision=highest)
    return jnp.stack([out_real, out_imag], axis=0) / jnp.sqrt(response)[None, :, :, None]


def shards(raw_samples, filter_taps, range_code, train_mask, steer_index):
    elem_dev = raw_samples.shape[0]
    gate_dev = raw_samples.shape[1]
    bin_dev = train_mask.shape[0]
    bin_total = bin_dev * lax.axis_size("dop")
    gates_total = gate_dev * lax.axis_size("rng")
    table = dft_table(bin_total)
    folded = raw_samples.astype(jnp.float32).reshape(elem_dev, gate_dev, 2, TAPS, CHANNELS)
    filtered = jnp.sum(folded * filter_taps, axis=3).astype(jnp.bfloat16)
    spectra = jnp.dot(
        filtered.reshape(elem_dev * gate_dev, 2 * CHANNELS),
        table,
        preferred_element_type=jnp.float32,
    )
    spectra = jnp.transpose(
        spectra.astype(jnp.bfloat16).reshape(elem_dev, gate_dev, 2, bin_total), (3, 1, 2, 0)
    )
    turned = lax.all_to_all(spectra, "dop", split_axis=0, concat_axis=3, tiled=True)
    padded = padded_2(turned, (("rng", 1),), CODE_REACH)
    compressed = compress(padded, range_code)
    masked = compressed * train_mask.astype(jnp.bfloat16)[:, :, None, None]
    dof_count = 2 * ELEMENTS
    identity = jnp.eye(dof_count, dtype=jnp.float32)
    steering = steering_table(steer_index)
    range_count = lax.axis_size("rng")
    owned_count = (bin_dev + range_count - 1) // range_count
    padded_bins = owned_count * range_count
    filled = jnp.pad(masked, ((0, padded_bins - bin_dev), (0, 0), (0, 0), (0, 0)))
    owned_rows = lax.all_to_all(filled, "rng", split_axis=0, concat_axis=1, tiled=True)
    owned_gram = local_gram(owned_rows) / gates_total + loading_level * identity
    owned_factor = jnp.linalg.cholesky(owned_gram)
    steer_filled = jnp.pad(steer_index, ((0, padded_bins - bin_dev), (0, 0)))
    first_bin = lax.axis_index("rng") * owned_count
    owned_steer = lax.dynamic_slice_in_dim(steer_filled, first_bin, owned_count, 0)
    owned_weights = solve_all(owned_factor, steering_table(owned_steer))
    weights = lax.all_gather(owned_weights, "rng", axis=0, tiled=True)[:bin_dev]
    return beam_output(compressed, weights, steering)


def solution(mesh):
    return jax.shard_map(
        shards,
        mesh=mesh,
        in_specs=(P("dop", "rng", None, None), P(), P(), P("dop", "rng"), P("dop", None)),
        out_specs=P(None, "dop", None, "rng"),
        check_vma=False,
    )
```

profile of v0, /device:TPU:0, one launch (start us, length us, event | category | flops | bytes accessed | tf_op | source)
XLA Modules:
  0.0 229.8 jit_solution(16720912339707050424)
XLA Ops:
  0.3 21.8 %reshape.482 = f32[32,24,2,8,512]{4,3,2,1,0:T(8,128)} reshape(bf16[32,24,2,4096]{3,2,1,0:T(2,128)(2,1)} %param.5) | data formatting | bytes 37748736 | tf_op jit(solution)/shard_map/reshape | solution.py:108
  22.1 15.0 %multiply_reduce_fusion = bf16[32,24,2,512]{3,2,1,0:T(2,128)(2,1)S(1)} fusion(f32[32,24,2,8,512]{4,3,2,1,0:T(8,128)} %reshape.482, f32[8,512]{1,0:T(8,128)S(1)} %copy-done.1), kind=kLoop, calls=%fused_computation.2 | loop fusion | flops 11796480 | bytes 26755072 | tf_op jit(solution)/shard_map/reduce_sum | solution.py:109
  38.7 0.8 reshape.483
  39.5 7.3 %all-to-all-start = ((bf16[8,2,1536]{2,1,0:T(2,128)(2,1)}), bf16[8,2,1536]{2,1,0:T(2,128)(2,1)S(1)}, u32[]{:S(2)}, u32[]{:S(2)}) async-start(bf16[8,2,1536]{2,1,0:T(2,128)(2,1)} %reshape.483), calls=%async_computation | async-start | bytes 98304 | tf_op jit(solution)/shard_map/all_to_all | solution.py:118
  47.1 6.5 %all-to-all-done = bf16[8,2,1536]{2,1,0:T(2,128)(2,1)S(1)} async-done(((bf16[8,2,1536]{2,1,0:T(2,128)(2,1)}), bf16[8,2,1536]{2,1,0:T(2,128)(2,1)S(1)}, u32[]{:S(2)}, u32[]{:S(2)}) %all-to-all-start) | async-done | bytes 49184 | tf_op jit(solution)/shard_map/all_to_all | solution.py:118
  54.0 1.3 collective-permute-start
  55.3 0.7 fusion.92
  56.0 1.3 collective-permute-start.1
  57.3 3.5 %collective-permute-done.1 = bf16[2,3,2,256]{3,1,2,0:T(4,128)(2,1)S(1)} collective-permute-done((bf16[2,3,2,256]{3,1,2,0:T(4,128)(2,1)S(1)}, bf16[2,3,2,256]{3,1,2,0:T(4,128)(2,1)S(1)}, u32[]{:S(2)}, u32[]{:S(2)}) %collective-permute-start.1) | collective-permute-done | bytes 6176 | tf_op jit(solution)/shard_map/ppermute | solution.py:25
  60.9 8.9 %add_convert_fusion = bf16[2,24,1,256]{3,1,2,0:T(8,128)(2,1)S(1)} fusion(f32[2,24,2,256]{3,1,2,0:T(8,128)S(1)} %get-tuple-element.36, f32[2,24,2,256]{3,1,2,0:T(8,128)S(1)} %get-tuple-element.37, f32[2,24,2,256]{3,1,2,0:T(8,128)S(1)} %get-tuple-element.35, f32[2,24,2,256]{3,1,2,0:T(8,128)S(1)} %get-tuple-element.42, ...), kind=kLoop, calls=%fused_computation.105 | loop fusion | flops 344064 | bytes 712760 | tf_op jit(solution)/shard_map/slice | solution.py:94
  69.7 8.9 %subtract_convert_fusion = bf16[2,24,1,256]{3,1,2,0:T(8,128)(2,1)S(1)} fusion(f32[2,24,2,256]{3,1,2,0:T(8,128)S(1)} %get-tuple-element.36, f32[2,24,2,256]{3,1,2,0:T(8,128)S(1)} %get-tuple-element.37, f32[2,24,2,256]{3,1,2,0:T(8,128)S(1)} %get-tuple-element.35, f32[2,24,2,256]{3,1,2,0:T(8,128)S(1)} %get-tuple-element.42, ...), kind=kLoop, calls=%fused_computation.106 | loop fusion | flops 344064 | bytes 712760 | tf_op jit(solution)/shard_map/slice | solution.py:93
  78.7 0.6 pad.9
  79.3 3.7 %all-to-all-start.1 = ((bf16[4,24,2,256]{3,1,2,0:T(8,128)(2,1)}), bf16[4,24,2,256]{3,1,2,0:T(8,128)(2,1)S(1)}, u32[]{:S(2)}, u32[]{:S(2)}) async-start(bf16[4,24,2,256]{3,1,2,0:T(8,128)(2,1)} %pad.9), calls=%async_computation.1 | async-start | bytes 196608 | tf_op jit(solution)/shard_map/all_to_all | solution.py:129
  83.0 4.3 %all-to-all-done.1 = bf16[4,24,2,256]{3,1,2,0:T(8,128)(2,1)S(1)} async-done(((bf16[4,24,2,256]{3,1,2,0:T(8,128)(2,1)}), bf16[4,24,2,256]{3,1,2,0:T(8,128)(2,1)S(1)}, u32[]{:S(2)}, u32[]{:S(2)}) %all-to-all-start.1) | async-done | bytes 98336 | tf_op jit(solution)/shard_map/all_to_all | solution.py:129
  88.3 11.7 %custom-call.38 = f32[1,128,128]{2,1,0:T(8,128)S(1)} custom-call(f32[1,128,128]{2,1,0:T(8,128)S(1)} %cholesky.267), custom_call_target="Cholesky" | custom-call | tf_op jit(solution)/shard_map/jit(cholesky)/cholesky | solution.py:131
  100.2 9.8 %custom-call.39 = f32[1,1,128,128]{2,3,1,0:T(8,128)S(1)} custom-call(f32[1,1,128,128]{3,2,1,0:T(8,128)S(1)} %get-tuple-element.34), custom_call_target="InvertDiagBlocksLowerTriangular" | custom-call | tf_op jit(solution)/shard_map/jit(cholesky)/cholesky | solution.py:131
  110.7 11.7 %custom-call.40 = f32[1,128,128]{2,1,0:T(8,128)S(1)} custom-call(f32[1,128,128]{2,1,0:T(8,128)S(1)} %cholesky.271), custom_call_target="Cholesky" | custom-call | tf_op jit(solution)/shard_map/jit(cholesky)/cholesky | solution.py:131
  122.4 10.0 %custom-call.41 = f32[1,1,128,128]{2,3,1,0:T(8,128)S(1)} custom-call(f32[1,1,128,128]{3,2,1,0:T(8,128)S(1)} %get-tuple-element.31), custom_call_target="InvertDiagBlocksLowerTriangular" | custom-call | tf_op jit(solution)/shard_map/jit(cholesky)/cholesky | solution.py:131
  133.1 11.7 %custom-call.42 = f32[1,128,128]{2,1,0:T(8,128)S(1)} custom-call(f32[1,128,128]{2,1,0:T(8,128)S(1)} %cholesky.276), custom_call_target="Cholesky" | custom-call | tf_op jit(solution)/shard_map/jit(cholesky)/cholesky | solution.py:131
  144.8 9.8 %custom-call.43 = f32[1,1,128,128]{2,3,1,0:T(8,128)S(1)} custom-call(f32[1,1,128,128]{3,2,1,0:T(8,128)S(1)} %get-tuple-element.28), custom_call_target="InvertDiagBlocksLowerTriangular" | custom-call | tf_op jit(solution)/shard_map/jit(cholesky)/cholesky | solution.py:131
  155.2 11.9 %custom-call.44 = f32[1,128,128]{2,1,0:T(8,128)S(1)} custom-call(f32[1,128,128]{2,1,0:T(8,128)S(1)} %fusion.5), custom_call_target="Cholesky" | custom-call | tf_op jit(solution)/shard_map/jit(cholesky)/cholesky | solution.py:131
  167.2 0.6 compare_reduce_fusion.3
  167.8 0.7 compare_reduce_fusion.2
  169.2 0.7 compare_reduce_fusion
  172.5 8.5 %while.1 = (s32[]{:T(128)}, f32[1,512,512]{2,1,0:T(8,128)S(1)}, s32[4,2]{0,1:T(2,128)S(1)}, f32[4,1,128,128]{3,2,1,0:T(8,128)S(1)}, s32[]{:T(128)}) while((s32[]{:T(128)}, f32[1,512,512]{2,1,0:T(8,128)S(1)}, s32[4,2]{0,1:T(2,128)S(1)}, f32[4,1,128,128]{3,2,1,0:T(8,128)S(1)}, s32[]{:T(128)}) %tuple.50), condition=%wide.while_cond, body=%wide.while_body.sunk | while | flops 2 | bytes 131189 | solution.py:82
  173.2 1.4 bitcast_dynamic-update-slice_fusion.2
  175.3 1.4 bitcast_dynamic-update-slice_fusion.2
  177.4 1.4 bitcast_dynamic-update-slice_fusion.2
  179.5 1.4 bitcast_dynamic-update-slice_fusion.2
  181.0 39.3 %custom-call.45 = f32[1,4,128,128]{2,3,1,0:T(8,128)S(1)} custom-call(f32[1,4,128,128]{3,2,1,0:T(8,128)S(1)} %bitcast.245), custom_call_target="InvertDiagBlocksLowerTriangular" | custom-call | tf_op jit(solution)/shard_map/vmap(jit(_cho_solve))/triangular_solve | solution.py:82
  223.3 5.2 %all_gather.3 = f32[4,512,4]{1,2,0:T(4,128)S(1)} all-gather(f32[1,512,4]{1,2,0:T(4,128)S(1)} %pad_maximum_fusion.1), channel_id=1, replica_groups=mesh['dop'=8,'rng'=4] {'rng'}, dimensions={0}, use_global_device_ids=true | all-gather | bytes 40960 | tf_op jit(solution)/shard_map/all_gather | solution.py:136
  229.1 0.7 maximum_divide_fusion
  (82 shorter events, 12.8 us)
Async XLA Ops:
  0.3 21.8 %copy-start.1 = (f32[8,512]{1,0:T(8,128)S(1)}, f32[8,512]{1,0:T(8,128)}, u32[]{:S(2)}) copy-start(f32[8,512]{1,0:T(8,128)} %param.6) | copy-start | bytes 49156
  37.5 9.2 %copy-start.2 = (s32[2,4]{1,0:T(2,128)S(1)}, s32[2,4]{1,0:T(2,128)}, u32[]{:S(2)}) copy-start(s32[2,4]{1,0:T(2,128)} %param.9) | copy-start | bytes 100
  37.5 17.7 %copy-start = (f32[2,7]{1,0:T(2,128)S(1)}, f32[2,7]{1,0:T(2,128)}, u32[]{:S(2)}) copy-start(f32[2,7]{1,0:T(2,128)} %param.7) | copy-start | bytes 172
  37.5 18.4 %copy-start.3 = (s32[2,24]{1,0:T(2,128)S(1)}, s32[2,24]{1,0:T(2,128)}, u32[]{:S(2)}) copy-start(s32[2,24]{1,0:T(2,128)} %param.8) | copy-start | bytes 580
  39.5 14.0 %all-to-all-start = ((bf16[8,2,1536]{2,1,0:T(2,128)(2,1)}), bf16[8,2,1536]{2,1,0:T(2,128)(2,1)S(1)}, u32[]{:S(2)}, u32[]{:S(2)}) async-start(bf16[8,2,1536]{2,1,0:T(2,128)(2,1)} %reshape.483), calls=%async_computation | async-start | bytes 98304 | tf_op jit(solution)/shard_map/all_to_all | solution.py:118
  54.0 3.3 %collective-permute-start = (bf16[2,3,2,256]{3,1,2,0:T(4,128)(2,1)S(1)}, bf16[2,3,2,256]{3,1,2,0:T(4,128)(2,1)S(1)}, u32[]{:S(2)}, u32[]{:S(2)}) collective-permute-start(bf16[2,3,2,256]{3,1,2,0:T(4,128)(2,1)S(1)} %get-tuple-element.43), channel_id=1, source_target_pairs={{0,1},{1,2},{2,3},{4,5},{5,6},{6,7},{8,9},{9,10},{10,11},{12,13},{... | collective-permute-start | bytes 18440 | tf_op jit(solution)/shard_map/ppermute | solution.py:24
  56.0 4.8 %collective-permute-start.1 = (bf16[2,3,2,256]{3,1,2,0:T(4,128)(2,1)S(1)}, bf16[2,3,2,256]{3,1,2,0:T(4,128)(2,1)S(1)}, u32[]{:S(2)}, u32[]{:S(2)}) collective-permute-start(bf16[2,3,2,256]{3,1,2,0:T(4,128)(2,1)S(1)} %get-tuple-element.44), channel_id=1, source_target_pairs={{1,0},{2,1},{3,2},{5,4},{6,5},{7,6},{9,8},{10,9},{11,10},{13,12},{... | collective-permute-start | bytes 18440 | tf_op jit(solution)/shard_map/ppermute | solution.py:25
  79.3 8.0 %all-to-all-start.1 = ((bf16[4,24,2,256]{3,1,2,0:T(8,128)(2,1)}), bf16[4,24,2,256]{3,1,2,0:T(8,128)(2,1)S(1)}, u32[]{:S(2)}, u32[]{:S(2)}) async-start(bf16[4,24,2,256]{3,1,2,0:T(8,128)(2,1)} %pad.9), calls=%async_computation.1 | async-start | bytes 196608 | tf_op jit(solution)/shard_map/all_to_all | solution.py:129
where the time goes:
time: 231 us; the launch traced here: 230 us
  other arithmetic  153 us (66%)
  local copies, waits for them, and re-layouts  34.2 us (15%)
  waiting for transfers between devices  14.2 us (6%)
  starting transfers between devices  13.5 us (6%)
  matrix products  6.22 us (3%)
  blocking collectives  5.21 us (2%)
  between operations  2.93 us (1%)
    another operation x15, other arithmetic, shards(): owned_factor = jnp.linalg.cholesky(owned_gram)  79.4 us
    another operation x4, other arithmetic, solve_all(): jax.scipy.linalg.cho_solve((lower_part, True), target)  39.5 us
    reshape x1, local copies, waits for them, and re-layouts, shards(): raw_samples.astype(jnp.float32)  21.8 us
    reduce_sum x1, other arithmetic, shards(): filtered = jnp.sum(folded * filter_taps, axis=3).astype(jnp.bfloat16)  15 us
    slice x1, other arithmetic, beam_output(): signal[:, :, 1]  8.88 us
    slice x1, other arithmetic, beam_output(): signal[:, :, 0]  8.88 us
    another operation x12, local copies, waits for them, and re-layouts  8.39 us
    all_to_all x1, starting transfers between devices, shards(): lax.all_to_all(spectra, 'dop', split_axis=0, concat_axis=3, tiled=True)  7.25 us
  transfers between devices with their start and end apart: 4, of which 3 were waited for; matrix products, arithmetic and copies ran while one was open for 0% of the time, Pallas kernels for 0%

commit v1 on v0

--- a/solution.py
+++ b/solution.py
@@ -3,6 +3,8 @@
 import jax
 import jax.numpy as jnp
 from jax import lax
+from jax.experimental import pallas as pl
+from jax.experimental.pallas import tpu as pltpu
 from jax.sharding import PartitionSpec as P
 
 ELEMENTS = 256
@@ -98,7 +100,7 @@
     return jnp.stack([out_real, out_imag], axis=0) / jnp.sqrt(response)[None, :, :, None]
 
 
-def shards(raw_samples, filter_taps, range_code, train_mask, steer_index):
+def plain_shards(raw_samples, filter_taps, range_code, train_mask, steer_index):
     elem_dev = raw_samples.shape[0]
     gate_dev = raw_samples.shape[1]
     bin_dev = train_mask.shape[0]
@@ -137,6 +139,345 @@
     return beam_output(compressed, weights, steering)
 
 
+LANES = 128
+MESH = pl.DeviceIdType.MESH
+NT = (((1,), (1,)), ((), ()))
+
+
+def pair_swapped(x, lane, slot):
+    imag = jnp.mod(lane // slot, 2) == 1
+    return jnp.where(imag, pltpu.roll(x, slot, 1), -pltpu.roll(x, LANES - slot, 1))
+
+
+def channelize_kernel(raw_ref, taps_ref, table_ref, out_ref, filt_ref, spec_ref):
+    elems, gates = raw_ref.shape[0], raw_ref.shape[1]
+    dops, rows = out_ref.shape[0], out_ref.shape[1]
+    step, steps = pl.program_id(0), pl.num_programs(0)
+    for gate in range(gates):
+
+        def one(e, carry, gate=gate):
+            x = raw_ref[e, gate].astype(jnp.float32).reshape(TAPS, 8, LANES)
+            at = pl.multiple_of((gate * elems + e) * 8, 8)
+            filt_ref[pl.ds(at, 8), :] = jnp.sum(x * taps_ref[...], axis=0)
+            return carry
+
+        lax.fori_loop(0, elems, one, 0, unroll=8)
+    parts = [
+        filt_ref[pl.ds(i, gates * elems, stride=8), :].astype(jnp.bfloat16) for i in range(8)
+    ]
+    chunk = lax.dot_general(
+        table_ref[...], jnp.concatenate(parts, axis=1), NT, preferred_element_type=jnp.float32
+    )
+    lane = lax.broadcasted_iota(jnp.int32, (dops, LANES), 1)
+    for q in range(gates):
+        row = jnp.zeros((dops, LANES), jnp.float32)
+        for c in range(LANES // elems):
+            piece = chunk[c * dops : (c + 1) * dops]
+            shift = ((c - q) * elems) % LANES
+            if shift:
+                piece = pltpu.roll(piece, shift, 1)
+            row = jnp.where(lane // elems == c, piece, row)
+        at = pl.multiple_of((step * gates + q) * dops, 8)
+        spec_ref[pl.ds(at, dops), :] = row
+
+    @pl.when(step == steps - 1)
+    def _():
+        full = steps * gates
+        if rows > full:
+            spec_ref[pl.ds(full * dops, (rows - full) * dops), :] = jnp.zeros(
+                ((rows - full) * dops, LANES), jnp.float32
+            )
+        for d in range(dops):
+            out_ref[d] = spec_ref[pl.ds(d, rows, stride=dops), :].astype(jnp.bfloat16)
+
+
+def channelize(raw, filter_taps, bin_total, dops, rows):
+    elems, gates = raw.shape[0], raw.shape[1]
+    bin_dev = bin_total // dops
+    quarters = CHANNELS // LANES
+    view = raw.reshape(elems, gates, 2, TAPS * quarters, LANES)
+    view = jnp.transpose(view, (0, 1, 3, 2, 4)).reshape(elems, gates, 2 * TAPS * quarters, LANES)
+    taps = filter_taps.reshape(TAPS, quarters, 1, LANES)
+    taps = jnp.broadcast_to(taps, (TAPS, quarters, 2, LANES)).reshape(TAPS, 2 * quarters, LANES)
+    table = dft_table(bin_total).reshape(2, quarters, LANES, 2, dops, bin_dev)
+    table = jnp.transpose(table, (5, 3, 4, 1, 0, 2)).reshape(2 * bin_total, 2 * CHANNELS)
+    block = LANES // elems
+    return pl.pallas_call(
+        channelize_kernel,
+        grid=(gates // block,),
+        in_specs=[
+            pl.BlockSpec((elems, block, 2 * TAPS * quarters, LANES), lambda i: (0, i, 0, 0)),
+            pl.BlockSpec(taps.shape, lambda i: (0, 0, 0)),
+            pl.BlockSpec(table.shape, lambda i: (0, 0)),
+        ],
+        out_specs=pl.BlockSpec((dops, rows, LANES), lambda i: (0, 0, 0)),
+        out_shape=jax.ShapeDtypeStruct((dops, rows, LANES), jnp.bfloat16),
+        scratch_shapes=[
+            pltpu.VMEM((elems * block * 8, LANES), jnp.float32),
+            pltpu.VMEM((rows * dops, LANES), jnp.float32),
+        ],
+        compiler_params=pltpu.CompilerParams(vmem_limit_bytes=56 * 1024 * 1024),
+    )(view, taps, table)
+
+
+def exchange_kernel(dops, rngs, spec_ref, mask_ref, out_ref, send1, recv1, send2, recv2):
+    d, r = lax.axis_index("dop"), lax.axis_index("rng")
+    barrier = pltpu.get_barrier_semaphore()
+    for i in range(1, dops):
+        pl.semaphore_signal(
+            barrier, inc=1, device_id=(lax.rem(d + i, dops), r), device_id_type=MESH
+        )
+    for j in range(1, rngs):
+        pl.semaphore_signal(
+            barrier, inc=1, device_id=(d, lax.rem(r + j, rngs)), device_id_type=MESH
+        )
+    pl.semaphore_wait(barrier, dops + rngs - 2)
+    out_ref[d, r] = spec_ref[d]
+    out_ref[dops, r] = mask_ref[...]
+    turns = []
+    for i in range(1, dops):
+        to = lax.rem(d + i, dops)
+        turns.append(
+            pltpu.make_async_remote_copy(
+                src_ref=spec_ref.at[to],
+                dst_ref=out_ref.at[d, r],
+                send_sem=send1.at[i],
+                recv_sem=recv1.at[i],
+                device_id=(to, r),
+                device_id_type=MESH,
+            )
+        )
+        turns[-1].start()
+    passed = []
+
+    def forward(block, i):
+        for j in range(1, rngs):
+            copy = pltpu.make_async_remote_copy(
+                src_ref=out_ref.at[block, r],
+                dst_ref=out_ref.at[block, r],
+                send_sem=send2.at[i, j],
+                recv_sem=recv2.at[i, j],
+                device_id=(d, lax.rem(r + j, rngs)),
+                device_id_type=MESH,
+            )
+            copy.start()
+            passed.append(copy)
+
+    forward(d, 0)
+    forward(dops, dops)
+    for i in range(1, dops):
+        turns[i - 1].wait_recv()
+        forward(lax.rem(d + dops - i, dops), i)
+    for copy in passed:
+        copy.wait_recv()
+    for copy in turns + passed:
+        copy.wait_send()
+
+
+def exchange(spectra, mask_rows, dops, rngs):
+    shape = (dops + 1, rngs) + mask_rows.shape
+    return pl.pallas_call(
+        lambda *refs: exchange_kernel(dops, rngs, *refs),
+        in_specs=[pl.BlockSpec(memory_space=pltpu.VMEM)] * 2,
+        out_specs=pl.BlockSpec(memory_space=pltpu.VMEM),
+        out_shape=jax.ShapeDtypeStruct(shape, jnp.bfloat16),
+        scratch_shapes=[
+            pltpu.SemaphoreType.DMA((dops,)),
+            pltpu.SemaphoreType.DMA((dops,)),
+            pltpu.SemaphoreType.DMA((dops + 1, rngs)),
+            pltpu.SemaphoreType.DMA((dops + 1, rngs)),
+        ],
+        compiler_params=pltpu.CompilerParams(collective_id=0, has_side_effects=True),
+    )(spectra, mask_rows)
+
+
+def eliminate(problems):
+    states = []
+    for a_re, a_im, b_re, b_im in problems:
+        size = a_re.shape[0]
+        tiles = [
+            [a_re[i : i + 8], a_im[i : i + 8]] for i in range(0, size, 8)
+        ] + [[b_re, b_im]]
+        states.append(tiles)
+    lanes = {
+        rows: lax.broadcasted_iota(jnp.int32, (rows, size), 1) for rows in (1, 8, b_re.shape[0])
+    }
+    for p in range(size):
+        first, s = divmod(p, 8)
+        for tiles in states:
+            row_re, row_im = (part[s : s + 1] for part in tiles[first])
+            inverse = 1.0 / row_re[:, p : p + 1]
+            here = lanes[1] == p
+            row_re = jnp.where(here, -inverse, row_re * inverse)
+            row_im = jnp.where(here, 0.0, row_im * inverse)
+            begin = first + 1 if s == 7 else first
+            for tile in tiles[begin:]:
+                t_re, t_im = tile
+                c_re, c_im = t_re[:, p : p + 1], t_im[:, p : p + 1]
+                at = lanes[t_re.shape[0]] == p
+                tile[0] = jnp.where(at, 0.0, t_re) - (c_re * row_re - c_im * row_im)
+                tile[1] = jnp.where(at, 0.0, t_im) - (c_re * row_im + c_im * row_re)
+    return [tiles[-1] for tiles in states]
+
+
+def adapt_kernel(gate_dev, bin_dev, code_ref, steer_ref, rows_ref, out_ref, self_ref, turned_ref):
+    dops, rngs = rows_ref.shape[0] - 1, rows_ref.shape[1]
+    gates = gate_dev * rngs
+    slot = LANES // (2 * bin_dev)
+    lane_dev = lax.broadcasted_iota(jnp.int32, (gate_dev, LANES), 1)
+    lane = lax.broadcasted_iota(jnp.int32, (gates, LANES), 1)
+    mask = jnp.concatenate(
+        [rows_ref[dops, r].astype(jnp.float32)[:gate_dev] for r in range(rngs)], axis=0
+    )
+    signal, turned, train, train_turned = [], [], [], []
+    edge = jnp.zeros((8, LANES), jnp.float32)
+    for d in range(dops):
+        for ref in (self_ref, turned_ref):
+            ref[d, 0:8] = edge
+            ref[d, 8 + gates : 16 + gates] = edge
+        for r in range(rngs):
+            y = rows_ref[d, r].astype(jnp.float32)[:gate_dev]
+            at = 8 + r * gate_dev
+            self_ref[d, at : at + gate_dev] = y
+            turned_ref[d, at : at + gate_dev] = pair_swapped(y, lane_dev, slot)
+        total = jnp.zeros((gates, LANES), jnp.float32)
+        for t in range(2 * CODE_REACH + 1):
+            at = 8 - CODE_REACH + t
+            total = (
+                total
+                + code_ref[0, t] * self_ref[d, at : at + gates]
+                + code_ref[1, t] * turned_ref[d, at : at + gates]
+            )
+        v = total.astype(jnp.bfloat16).astype(jnp.float32)
+        q = pair_swapped(v, lane, slot)
+        signal.append(v.astype(jnp.bfloat16))
+        turned.append(q.astype(jnp.bfloat16))
+        train.append((v * mask).astype(jnp.bfloat16))
+        train_turned.append((q * mask).astype(jnp.bfloat16))
+
+    def dot(a, b):
+        return lax.dot_general(a, b, NT, preferred_element_type=jnp.float32)
+
+    def of_bins(parts):
+        rows = []
+        for k in range(bin_dev):
+            own = lane // (2 * slot) == k
+            rows.append(
+                jnp.concatenate(
+                    [jnp.where(own, x.astype(jnp.float32), 0.0).astype(jnp.bfloat16) for x in parts],
+                    axis=1,
+                )
+            )
+        return jnp.concatenate(rows, axis=0)
+
+    signal_bins, train_bins = of_bins(signal), of_bins(train)
+    signal, turned, train, train_turned = (
+        jnp.concatenate(x, axis=1) for x in (signal, turned, train, train_turned)
+    )
+    all_re, all_im = dot(signal_bins, signal), dot(signal_bins, turned)
+    gram_re, gram_im = dot(train_bins, train), dot(train_bins, train_turned)
+    steer = steer_ref[...]
+    high = steer.astype(jnp.bfloat16)
+    rest = steer - high.astype(jnp.float32)
+    middle = rest.astype(jnp.bfloat16)
+    low = (rest - middle.astype(jnp.float32)).astype(jnp.bfloat16)
+    looks = dot(high, signal) + (dot(middle, signal) + dot(low, signal))
+    sights = dot(high, train) + (dot(middle, train) + dot(low, train))
+    norms = jnp.sum(steer * steer, axis=1, keepdims=True)
+    beams = steer.shape[0] // (2 * bin_dev)
+    diagonal = (
+        lax.broadcasted_iota(jnp.int32, (gates, gates), 0)
+        == lax.broadcasted_iota(jnp.int32, (gates, gates), 1)
+    )
+    loading = jnp.where(diagonal, loading_level * gates, 0.0)
+    problems = []
+    for k in range(bin_dev):
+        at, b = k * gates, 2 * k * beams
+        problems.append(
+            (
+                gram_re[at : at + gates] + loading,
+                -gram_im[at : at + gates],
+                sights[b : b + beams],
+                sights[b + beams : b + 2 * beams],
+            )
+        )
+    solved = eliminate(problems)
+    place = lax.axis_index("rng")
+    highest = lax.Precision.HIGHEST
+    for k in range(bin_dev):
+        y_re, y_im = solved[k]
+        b_re, b_im = problems[k][2:]
+        at, b = k * gates, 2 * k * beams
+        k_re, k_im = all_re[at : at + gates], all_im[at : at + gates]
+        both = jnp.concatenate([y_re, y_im], axis=0)
+        by_re = jnp.dot(both, k_re, precision=highest, preferred_element_type=jnp.float32)
+        by_im = jnp.dot(both, k_im, precision=highest, preferred_element_type=jnp.float32)
+        o_re = looks[b : b + beams] - (by_re[:beams] + by_im[beams:])
+        o_im = looks[b + beams : b + 2 * beams] - (by_re[beams:] - by_im[:beams])
+        lost = jnp.sum(b_re * y_re + b_im * y_im, axis=1, keepdims=True)
+        response = (norms[b : b + beams] - lost) / loading_level
+        scale = 1.0 / (loading_level * jnp.sqrt(response))
+        for part, o in enumerate((o_re, o_im)):
+            o = o * scale
+            mine = o[:, :gate_dev]
+            for r in range(1, rngs):
+                mine = jnp.where(place == r, o[:, r * gate_dev : (r + 1) * gate_dev], mine)
+            out_ref[part, k] = mine
+
+
+def steering_rows(steer_index, dops, slot):
+    bin_dev, beams = steer_index.shape
+    steering = jnp.transpose(steering_table(steer_index), (0, 2, 1))
+    cosine = steering[:, :, :ELEMENTS].reshape(bin_dev, beams, dops, 1, slot)
+    sine_part = steering[:, :, ELEMENTS:].reshape(bin_dev, beams, dops, 1, slot)
+    real_rows = jnp.concatenate([cosine, sine_part], axis=3)
+    imag_rows = jnp.concatenate([-sine_part, cosine], axis=3)
+    rows = jnp.stack([real_rows, imag_rows], axis=1)
+    own = jnp.eye(bin_dev, dtype=jnp.float32)[:, None, None, None, :, None, None]
+    return (rows[:, :, :, :, None] * own).reshape(2 * bin_dev * beams, dops * LANES)
+
+
+def adapt(rows, range_code, steer, gate_dev, bin_dev):
+    dops, rngs = rows.shape[0] - 1, rows.shape[1]
+    gates = gate_dev * rngs
+    beams = steer.shape[0] // (2 * bin_dev)
+    vmem = pl.BlockSpec(memory_space=pltpu.VMEM)
+    return pl.pallas_call(
+        lambda *refs: adapt_kernel(gate_dev, bin_dev, *refs),
+        in_specs=[pl.BlockSpec(memory_space=pltpu.SMEM), vmem, vmem],
+        out_specs=vmem,
+        out_shape=jax.ShapeDtypeStruct((2, bin_dev, beams, gate_dev), jnp.float32),
+        scratch_shapes=[pltpu.VMEM((dops, gates + 16, LANES), jnp.float32)] * 2,
+        compiler_params=pltpu.CompilerParams(vmem_limit_bytes=32 * 1024 * 1024),
+    )(range_code, steer, rows)
+
+
+def dual_shards(raw_samples, filter_taps, range_code, train_mask, steer_index):
+    elem_dev, gate_dev = raw_samples.shape[:2]
+    bin_dev = train_mask.shape[0]
+    dops, rngs = lax.axis_size("dop"), lax.axis_size("rng")
+    rows = -(-gate_dev // 16) * 16
+    spectra = channelize(raw_samples, filter_taps, bin_dev * dops, dops, rows)
+    mask_rows = jnp.repeat(jnp.transpose(train_mask), LANES // bin_dev, axis=1)
+    mask_rows = jnp.pad(mask_rows.astype(jnp.bfloat16), ((0, rows - gate_dev), (0, 0)))
+    gathered = exchange(spectra, mask_rows, dops, rngs)
+    steer = steering_rows(steer_index, dops, elem_dev)
+    return adapt(gathered, range_code, steer, gate_dev, bin_dev)
+
+
+def shards(raw_samples, filter_taps, range_code, train_mask, steer_index):
+    elem_dev, gate_dev = raw_samples.shape[:2]
+    dops, rngs = lax.axis_size("dop"), lax.axis_size("rng")
+    fits = (
+        2 * train_mask.shape[0] * elem_dev == LANES
+        and dops == 8
+        and gate_dev % 8 == 0
+        and gate_dev * rngs <= LANES
+    )
+    path = dual_shards if fits else plain_shards
+    return path(raw_samples, filter_taps, range_code, train_mask, steer_index)
+
+
 def solution(mesh):
     return jax.shard_map(
         shards,

time: 231 us -> 42.4 us (0.18)
  other arithmetic: 153 us -> 1.61 us
  Pallas kernels: 0 us -> 35.9 us
  local copies, waits for them, and re-layouts: 34.2 us -> 4.43 us
  waiting for transfers between devices: 14.2 us -> 0 us
  starting transfers between devices: 13.5 us -> 0 us
  matrix products: 6.22 us -> 0 us
  blocking collectives: 5.21 us -> 0 us
  between operations: 2.93 us -> 0.14 us
    another operation x21 -> x4, other arithmetic: 119 us -> 0.49 us  [the longest x15 79.4 us: shards(): owned_factor = jnp.linalg.cholesky(owned_gram)]
    pallas_call x0 -> x3, Pallas kernels: none -> 35.9 us  [the longest x1 14.7 us: exchange(): pl.pallas_call(lambda *refs: exchange_kernel(dops, rngs, *refs), in_specs...]
    reshape x2, local copies, waits for them, and re-layouts: 22.2 us -> 0.21 us  [the longest x1 0.11 us: steering_rows(): sine_part = steering[:, :, ELEMENTS:].reshape(bin_dev, beams, dops, 1, slot)]
    slice x2 -> x0, other arithmetic: 17.8 us -> none  [the longest x1 8.88 us: beam_output(): signal[:, :, 1]]
    reduce_sum x2 -> x0, other arithmetic: 15.1 us -> none  [the longest x1 15 us: shards(): filtered = jnp.sum(folded * filter_taps, axis=3).astype(jnp.bfloat16)]
    all_to_all x2 -> x0, starting transfers between devices: 10.9 us -> none  [the longest x1 7.25 us: shards(): lax.all_to_all(spectra, 'dop', split_axis=0, concat_axis=3, tiled=True)]
    all_to_all x2 -> x0, waiting for transfers between devices: 10.8 us -> none  [the longest x1 6.47 us: shards(): lax.all_to_all(spectra, 'dop', split_axis=0, concat_axis=3, tiled=True)]
    another operation x17 -> x0, local copies, waits for them, and re-layouts: 8.54 us -> none
  transfers between devices with their start and end apart: 4 -> 0, of which waited for: 3 -> 0; matrix products, arithmetic and copies ran while one was open for 0% -> 0% of each run, Pallas kernels for 0% -> 0%
where the time goes in v1:
time: 42.4 us; the launch traced here: 42 us
  Pallas kernels  35.9 us (85%)
  local copies, waits for them, and re-layouts  4.43 us (10%)
  other arithmetic  1.61 us (4%)
    pallas_call x1, Pallas kernels, exchange(): pl.pallas_call(lambda *refs: exchange_kernel(dops, rngs, *refs), in_specs...  14.7 us
    pallas_call x1, Pallas kernels, adapt(): pl.pallas_call(lambda *refs: adapt_kernel(gate_dev, bin_dev, *refs), in_s...  12.3 us
    pallas_call x1, Pallas kernels, channelize(): pl.pallas_call(channelize_kernel, grid=(gates // block,), in_specs=[pl.Bl...  8.82 us
    broadcast_in_dim x2, local copies, waits for them, and re-layouts, channelize(): jnp.broadcast_to(taps, (TAPS, quarters, 2, LANES))  1.35 us
    unnamed x6, local copies, waits for them, and re-layouts  0.96 us

profile of v1, /device:TPU:0, one launch (start us, length us, event | category | flops | bytes accessed | tf_op | source)
XLA Modules:
  0.0 42.0 jit_solution(20228807653792091)
XLA Ops:
  0.0 0.0 copy-start.2
  0.0 0.0 copy-start.1
  0.0 0.7 %multiply_add_fusion = s32[2,4]{1,0:T(2,128)S(1)} fusion(s32[2,4]{1,0:T(2,128)} %param.9), kind=kLoop, calls=%fused_computation.28 | loop fusion | flops 16 | bytes 64 | tf_op jit(solution)/shard_map/sub | solution.py:76
  0.7 0.2 fusion.11
  0.9 0.1 reshape.54
  1.1 0.1 reshape.53
  1.2 0.1 maximum_bitcast_fusion
  1.3 0.1 pad_maximum_fusion
  1.4 0.2 broadcast_multiply_fusion
  1.6 0.3 mul.92.refs_1_
  1.9 0.1 negate_convert_fusion
  2.1 0.1 fusion.6
  2.3 0.6 %copy.13 = bf16[2,2,8,4,2,128]{5,2,4,3,1,0:T(8,128)(2,1)} copy(bf16[2,2,8,4,2,128]{5,3,4,0,2,1:T(4,128)(2,1)S(1)} %bitcast.23) | data formatting | bytes 131072 | tf_op jit(solution)/shard_map/transpose | solution.py:203
  2.9 0.7 %copy.12 = f32[8,4,128]{2,1,0:T(4,128)S(1)} copy(f32[8,4,128]{2,0,1:T(8,128)} %bitcast.25) | data formatting | bytes 32768 | tf_op jit(solution)/shard_map/broadcast_in_dim | solution.py:201
  3.7 0.6 %broadcast_in_dim.7 = f32[8,4,2,128]{3,2,1,0:T(2,128)} broadcast(f32[8,4,128]{2,1,0:T(4,128)S(1)} %copy.12), dimensions={0,1,3} | broadcast | bytes 49152 | tf_op jit(solution)/shard_map/broadcast_in_dim | solution.py:201
  4.3 8.8 %shard_map.55.refs_0_ = bf16[8,32,128]{2,1,0:T(8,128)(2,1)} custom-call(bf16[32,24,64,128]{3,2,1,0:T(8,128)(2,1)} %bitcast.21, f32[8,8,128]{2,1,0:T(8,128)} %bitcast.24, bf16[32,1024]{1,0:T(8,128)(2,1)} %bitcast.22), custom_call_target="tpu_custom_call" | custom-call | tf_op jit(solution)/shard_map/pallas_call | solution.py:205
  13.1 0.0 copy-done.2
  13.1 0.1 copy.14
  13.2 0.1 broadcast_in_dim.8
  13.3 0.1 convert_element_type.42
  13.4 0.6 %pad.4.refs_1_ = bf16[32,128]{1,0:T(8,128)(2,1)} pad(bf16[24,128]{1,0:T(8,128)(2,1)S(1)} %convert_element_type.42, bf16[]{:T(256)} %constant.37.clone.1), padding=0_8x0_0 | pad | bytes 14338 | tf_op jit(solution)/shard_map/jit(_pad)/pad | solution.py:462
  14.0 14.7 %shard_map.56.refs_2_ = bf16[9,4,32,128]{3,2,1,0:T(8,128)(2,1)} custom-call(bf16[8,32,128]{2,1,0:T(8,128)(2,1)} %shard_map.55.refs_0_, bf16[32,128]{1,0:T(8,128)(2,1)} %pad.4.refs_1_), custom_call_target="tpu_custom_call" | custom-call | tf_op jit(solution)/shard_map/pallas_call | solution.py:279
  28.7 0.0 copy-done.1
  28.7 0.0 copy-start
  28.8 1.0 %copy-done = bf16[9,4,32,128]{3,2,1,0:T(8,128)(2,1)S(1)} copy-done((bf16[9,4,32,128]{3,2,1,0:T(8,128)(2,1)S(1)}, bf16[9,4,32,128]{3,2,1,0:T(8,128)(2,1)}, u32[]{:S(2)}) %copy-start) | copy-done | bytes 294936
  29.7 12.3 %shard_map.57 = f32[2,2,4,24]{3,2,1,0:T(4,128)} custom-call(f32[2,7]{1,0:T(2,128)S(1)} %copy-done.1, f32[16,1024]{1,0:T(8,128)S(1)} %mul.92.refs_1_, bf16[9,4,32,128]{3,2,1,0:T(8,128)(2,1)S(1)} %copy-done), custom_call_target="tpu_custom_call" | custom-call | tf_op jit(solution)/shard_map/pallas_call | solution.py:445
  (7 shorter events, 0.1 us)
Async XLA Ops:
  0.0 13.1 %copy-start.2 = (s32[2,24]{1,0:T(2,128)S(1)}, s32[2,24]{1,0:T(2,128)}, u32[]{:S(2)}) copy-start(s32[2,24]{1,0:T(2,128)} %param.8) | copy-start | bytes 580
  0.0 28.7 %copy-start.1 = (f32[2,7]{1,0:T(2,128)S(1)}, f32[2,7]{1,0:T(2,128)}, u32[]{:S(2)}) copy-start(f32[2,7]{1,0:T(2,128)} %refs_0_.1) | copy-start | bytes 172
  28.7 1.0 %copy-start = (bf16[9,4,32,128]{3,2,1,0:T(8,128)(2,1)S(1)}, bf16[9,4,32,128]{3,2,1,0:T(8,128)(2,1)}, u32[]{:S(2)}) copy-start(bf16[9,4,32,128]{3,2,1,0:T(8,128)(2,1)} %shard_map.56.refs_2_) | copy-start | bytes 884740

commit v2 on v1

--- a/solution.py
+++ b/solution.py
@@ -2,6 +2,8 @@
 
 import jax
 import jax.numpy as jnp
+import ml_dtypes
+import numpy as np
 from jax import lax
 from jax.experimental import pallas as pl
 from jax.experimental.pallas import tpu as pltpu
@@ -149,16 +151,26 @@
     return jnp.where(imag, pltpu.roll(x, slot, 1), -pltpu.roll(x, LANES - slot, 1))
 
 
-def channelize_kernel(raw_ref, taps_ref, table_ref, out_ref, filt_ref, spec_ref):
+def channelize_kernel(raw_ref, taps_ref, table_ref, mask_ref, out_ref, filt_ref, spec_ref):
     elems, gates = raw_ref.shape[0], raw_ref.shape[1]
-    dops, rows = out_ref.shape[0], out_ref.shape[1]
+    dops, rows = out_ref.shape[0] - 1, out_ref.shape[1]
     step, steps = pl.program_id(0), pl.num_programs(0)
+    taps = []
+    for t in range(TAPS):
+        quarters = [
+            jnp.broadcast_to(taps_ref[t : t + 1, i : i + LANES], (2, LANES))
+            for i in range(0, CHANNELS, LANES)
+        ]
+        taps.append(jnp.concatenate(quarters, axis=0))
     for gate in range(gates):
 
         def one(e, carry, gate=gate):
-            x = raw_ref[e, gate].astype(jnp.float32).reshape(TAPS, 8, LANES)
+            x = raw_ref[e, gate].astype(jnp.float32)
+            terms = [x[8 * t : 8 * t + 8] * taps[t] for t in range(TAPS)]
+            while len(terms) > 1:
+                terms = [a + b for a, b in zip(terms[::2], terms[1::2])]
             at = pl.multiple_of((gate * elems + e) * 8, 8)
-            filt_ref[pl.ds(at, 8), :] = jnp.sum(x * taps_ref[...], axis=0)
+            filt_ref[pl.ds(at, 8), :] = terms[0]
             return carry
 
         lax.fori_loop(0, elems, one, 0, unroll=8)
@@ -189,38 +201,59 @@
             )
         for d in range(dops):
             out_ref[d] = spec_ref[pl.ds(d, rows, stride=dops), :].astype(jnp.bfloat16)
-
-
-def channelize(raw, filter_taps, bin_total, dops, rows):
+        bins, own = mask_ref.shape
+        held = mask_ref[...].astype(jnp.float32)
+        lane = lax.broadcasted_iota(jnp.int32, (bins, LANES), 1)
+        bin_row = lax.broadcasted_iota(jnp.int32, (bins, LANES), 0)
+        spread = jnp.where(lane // (LANES // bins) == bin_row, 1.0, 0.0)
+        column = lax.dot_general(
+            held, spread, (((0,), (0,)), ((), ())), preferred_element_type=jnp.float32
+        )
+        column = jnp.concatenate([column, jnp.zeros((rows - own, LANES), jnp.float32)], axis=0)
+        out_ref[dops] = column.astype(jnp.bfloat16)
+
+
+def constant_table(bin_total):
+    mode_index, bin_index = np.arange(CHANNELS), np.arange(bin_total)
+    turn_count = np.mod(mode_index[:, None] * bin_index[None, :], CHANNELS).astype(np.float32)
+    phases = turn_count * np.float32(2.0 * math.pi / CHANNELS)
+    cosine = np.cos(phases) / np.float32(math.sqrt(CHANNELS))
+    sine_part = np.sin(phases) / np.float32(math.sqrt(CHANNELS))
+    table = np.block([[cosine, -sine_part], [sine_part, cosine]])
+    return table.astype(ml_dtypes.bfloat16)
+
+
+def channelize(raw, filter_taps, train_mask, bin_total, dops, rows):
     elems, gates = raw.shape[0], raw.shape[1]
     bin_dev = bin_total // dops
     quarters = CHANNELS // LANES
     view = raw.reshape(elems, gates, 2, TAPS * quarters, LANES)
     view = jnp.transpose(view, (0, 1, 3, 2, 4)).reshape(elems, gates, 2 * TAPS * quarters, LANES)
-    taps = filter_taps.reshape(TAPS, quarters, 1, LANES)
-    taps = jnp.broadcast_to(taps, (TAPS, quarters, 2, LANES)).reshape(TAPS, 2 * quarters, LANES)
-    table = dft_table(bin_total).reshape(2, quarters, LANES, 2, dops, bin_dev)
-    table = jnp.transpose(table, (5, 3, 4, 1, 0, 2)).reshape(2 * bin_total, 2 * CHANNELS)
+    table = constant_table(bin_total).reshape(2, quarters, LANES, 2, dops, bin_dev)
+    table = jnp.asarray(
+        np.transpose(table, (5, 3, 4, 1, 0, 2)).reshape(2 * bin_total, 2 * CHANNELS)
+    )
     block = LANES // elems
     return pl.pallas_call(
         channelize_kernel,
         grid=(gates // block,),
         in_specs=[
             pl.BlockSpec((elems, block, 2 * TAPS * quarters, LANES), lambda i: (0, i, 0, 0)),
-            pl.BlockSpec(taps.shape, lambda i: (0, 0, 0)),
+            pl.BlockSpec(filter_taps.shape, lambda i: (0, 0)),
             pl.BlockSpec(table.shape, lambda i: (0, 0)),
+            pl.BlockSpec(train_mask.shape, lambda i: (0, 0)),
         ],
-        out_specs=pl.BlockSpec((dops, rows, LANES), lambda i: (0, 0, 0)),
-        out_shape=jax.ShapeDtypeStruct((dops, rows, LANES), jnp.bfloat16),
+        out_specs=pl.BlockSpec((dops + 1, rows, LANES), lambda i: (0, 0, 0)),
+        out_shape=jax.ShapeDtypeStruct((dops + 1, rows, LANES), jnp.bfloat16),
         scratch_shapes=[
             pltpu.VMEM((elems * block * 8, LANES), jnp.float32),
             pltpu.VMEM((rows * dops, LANES), jnp.float32),
         ],
         compiler_params=pltpu.CompilerParams(vmem_limit_bytes=56 * 1024 * 1024),
-    )(view, taps, table)
-
-
-def exchange_kernel(dops, rngs, spec_ref, mask_ref, out_ref, send1, recv1, send2, recv2):
+    )(view, filter_taps, table, train_mask)
+
+
+def exchange_kernel(dops, rngs, spec_ref, out_ref, send1, recv1, send2, recv2):
     d, r = lax.axis_index("dop"), lax.axis_index("rng")
     barrier = pltpu.get_barrier_semaphore()
     for i in range(1, dops):
@@ -232,15 +265,13 @@
             barrier, inc=1, device_id=(d, lax.rem(r + j, rngs)), device_id_type=MESH
         )
     pl.semaphore_wait(barrier, dops + rngs - 2)
-    out_ref[d, r] = spec_ref[d]
-    out_ref[dops, r] = mask_ref[...]
     turns = []
     for i in range(1, dops):
         to = lax.rem(d + i, dops)
         turns.append(
             pltpu.make_async_remote_copy(
                 src_ref=spec_ref.at[to],
-                dst_ref=out_ref.at[d, r],
+                dst_ref=out_ref.at[r, d],
                 send_sem=send1.at[i],
                 recv_sem=recv1.at[i],
                 device_id=(to, r),
@@ -248,47 +279,43 @@
             )
         )
         turns[-1].start()
+    out_ref[r, d] = spec_ref[d]
+    out_ref[r, dops] = spec_ref[dops]
+    for copy in turns:
+        copy.wait_recv()
     passed = []
-
-    def forward(block, i):
-        for j in range(1, rngs):
-            copy = pltpu.make_async_remote_copy(
-                src_ref=out_ref.at[block, r],
-                dst_ref=out_ref.at[block, r],
-                send_sem=send2.at[i, j],
-                recv_sem=recv2.at[i, j],
-                device_id=(d, lax.rem(r + j, rngs)),
-                device_id_type=MESH,
-            )
-            copy.start()
-            passed.append(copy)
-
-    forward(d, 0)
-    forward(dops, dops)
-    for i in range(1, dops):
-        turns[i - 1].wait_recv()
-        forward(lax.rem(d + dops - i, dops), i)
+    for j in range(1, rngs):
+        copy = pltpu.make_async_remote_copy(
+            src_ref=out_ref.at[r],
+            dst_ref=out_ref.at[r],
+            send_sem=send2.at[j],
+            recv_sem=recv2.at[j],
+            device_id=(d, lax.rem(r + j, rngs)),
+            device_id_type=MESH,
+        )
+        copy.start()
+        passed.append(copy)
     for copy in passed:
         copy.wait_recv()
     for copy in turns + passed:
         copy.wait_send()
 
 
-def exchange(spectra, mask_rows, dops, rngs):
-    shape = (dops + 1, rngs) + mask_rows.shape
+def exchange(spectra, rngs):
+    dops = spectra.shape[0] - 1
     return pl.pallas_call(
         lambda *refs: exchange_kernel(dops, rngs, *refs),
-        in_specs=[pl.BlockSpec(memory_space=pltpu.VMEM)] * 2,
+        in_specs=[pl.BlockSpec(memory_space=pltpu.VMEM)],
         out_specs=pl.BlockSpec(memory_space=pltpu.VMEM),
-        out_shape=jax.ShapeDtypeStruct(shape, jnp.bfloat16),
+        out_shape=jax.ShapeDtypeStruct((rngs,) + spectra.shape, jnp.bfloat16),
         scratch_shapes=[
             pltpu.SemaphoreType.DMA((dops,)),
             pltpu.SemaphoreType.DMA((dops,)),
-            pltpu.SemaphoreType.DMA((dops + 1, rngs)),
-            pltpu.SemaphoreType.DMA((dops + 1, rngs)),
+            pltpu.SemaphoreType.DMA((rngs,)),
+            pltpu.SemaphoreType.DMA((rngs,)),
         ],
         compiler_params=pltpu.CompilerParams(collective_id=0, has_side_effects=True),
-    )(spectra, mask_rows)
+    )(spectra)
 
 
 def eliminate(problems):
@@ -302,32 +329,48 @@
     lanes = {
         rows: lax.broadcasted_iota(jnp.int32, (rows, size), 1) for rows in (1, 8, b_re.shape[0])
     }
-    for p in range(size):
+    for p in range(0, size, 2):
         first, s = divmod(p, 8)
         for tiles in states:
-            row_re, row_im = (part[s : s + 1] for part in tiles[first])
-            inverse = 1.0 / row_re[:, p : p + 1]
-            here = lanes[1] == p
-            row_re = jnp.where(here, -inverse, row_re * inverse)
-            row_im = jnp.where(here, 0.0, row_im * inverse)
-            begin = first + 1 if s == 7 else first
+            u_re, u_im = (part[s : s + 1] for part in tiles[first])
+            v_re, v_im = (part[s + 1 : s + 2] for part in tiles[first])
+            a, c = u_re[:, p : p + 1], v_re[:, p + 1 : p + 2]
+            b_re, b_im = u_re[:, p + 1 : p + 2], u_im[:, p + 1 : p + 2]
+            inverse = 1.0 / (a * c - (b_re * b_re + b_im * b_im))
+            a, c, b_re, b_im = a * inverse, c * inverse, b_re * inverse, b_im * inverse
+            one, two = lanes[1] == p, lanes[1] == p + 1
+            pair = one | two
+            u_re = jnp.where(pair, jnp.where(one, -1.0, 0.0), u_re)
+            v_re = jnp.where(pair, jnp.where(two, -1.0, 0.0), v_re)
+            u_im, v_im = jnp.where(pair, 0.0, u_im), jnp.where(pair, 0.0, v_im)
+            f_re = c * u_re - (b_re * v_re - b_im * v_im)
+            f_im = c * u_im - (b_re * v_im + b_im * v_re)
+            g_re = a * v_re - (b_re * u_re + b_im * u_im)
+            g_im = a * v_im - (b_re * u_im - b_im * u_re)
+            begin = first + 1 if s == 6 else first
             for tile in tiles[begin:]:
                 t_re, t_im = tile
-                c_re, c_im = t_re[:, p : p + 1], t_im[:, p : p + 1]
-                at = lanes[t_re.shape[0]] == p
-                tile[0] = jnp.where(at, 0.0, t_re) - (c_re * row_re - c_im * row_im)
-                tile[1] = jnp.where(at, 0.0, t_im) - (c_re * row_im + c_im * row_re)
+                x_re, x_im = t_re[:, p : p + 1], t_im[:, p : p + 1]
+                y_re, y_im = t_re[:, p + 1 : p + 2], t_im[:, p + 1 : p + 2]
+                at = lanes[t_re.shape[0]]
+                keep = (at != p) & (at != p + 1)
+                tile[0] = jnp.where(keep, t_re, 0.0) - (
+                    (x_re * f_re - x_im * f_im) + (y_re * g_re - y_im * g_im)
+                )
+                tile[1] = jnp.where(keep, t_im, 0.0) - (
+                    (x_re * f_im + x_im * f_re) + (y_re * g_im + y_im * g_re)
+                )
     return [tiles[-1] for tiles in states]
 
 
 def adapt_kernel(gate_dev, bin_dev, code_ref, steer_ref, rows_ref, out_ref, self_ref, turned_ref):
-    dops, rngs = rows_ref.shape[0] - 1, rows_ref.shape[1]
+    rngs, dops = rows_ref.shape[0], rows_ref.shape[1] - 1
     gates = gate_dev * rngs
     slot = LANES // (2 * bin_dev)
     lane_dev = lax.broadcasted_iota(jnp.int32, (gate_dev, LANES), 1)
     lane = lax.broadcasted_iota(jnp.int32, (gates, LANES), 1)
     mask = jnp.concatenate(
-        [rows_ref[dops, r].astype(jnp.float32)[:gate_dev] for r in range(rngs)], axis=0
+        [rows_ref[r, dops].astype(jnp.float32)[:gate_dev] for r in range(rngs)], axis=0
     )
     signal, turned, train, train_turned = [], [], [], []
     edge = jnp.zeros((8, LANES), jnp.float32)
@@ -336,7 +379,7 @@
             ref[d, 0:8] = edge
             ref[d, 8 + gates : 16 + gates] = edge
         for r in range(rngs):
-            y = rows_ref[d, r].astype(jnp.float32)[:gate_dev]
+            y = rows_ref[r, d].astype(jnp.float32)[:gate_dev]
             at = 8 + r * gate_dev
             self_ref[d, at : at + gate_dev] = y
             turned_ref[d, at : at + gate_dev] = pair_swapped(y, lane_dev, slot)
@@ -345,8 +388,8 @@
             at = 8 - CODE_REACH + t
             total = (
                 total
-                + code_ref[0, t] * self_ref[d, at : at + gates]
-                + code_ref[1, t] * turned_ref[d, at : at + gates]
+                + code_ref[0:1, t : t + 1] * self_ref[d, at : at + gates]
+                + code_ref[1:2, t : t + 1] * turned_ref[d, at : at + gates]
             )
         v = total.astype(jnp.bfloat16).astype(jnp.float32)
         q = pair_swapped(v, lane, slot)
@@ -376,7 +419,7 @@
     )
     all_re, all_im = dot(signal_bins, signal), dot(signal_bins, turned)
     gram_re, gram_im = dot(train_bins, train), dot(train_bins, train_turned)
-    steer = steer_ref[...]
+    steer = steering_rows(steer_ref[...], dops, slot)
     high = steer.astype(jnp.bfloat16)
     rest = steer - high.astype(jnp.float32)
     middle = rest.astype(jnp.bfloat16)
@@ -426,25 +469,36 @@
 
 
 def steering_rows(steer_index, dops, slot):
-    bin_dev, beams = steer_index.shape
-    steering = jnp.transpose(steering_table(steer_index), (0, 2, 1))
-    cosine = steering[:, :, :ELEMENTS].reshape(bin_dev, beams, dops, 1, slot)
-    sine_part = steering[:, :, ELEMENTS:].reshape(bin_dev, beams, dops, 1, slot)
-    real_rows = jnp.concatenate([cosine, sine_part], axis=3)
-    imag_rows = jnp.concatenate([-sine_part, cosine], axis=3)
-    rows = jnp.stack([real_rows, imag_rows], axis=1)
-    own = jnp.eye(bin_dev, dtype=jnp.float32)[:, None, None, None, :, None, None]
-    return (rows[:, :, :, :, None] * own).reshape(2 * bin_dev * beams, dops * LANES)
+    bins, beams = steer_index.shape
+    looks = [
+        jnp.broadcast_to(steer_index[k : k + 1, j : j + 1], (1, LANES))
+        for k in range(bins)
+        for _ in range(2)
+        for j in range(beams)
+    ]
+    look = 2 * jnp.concatenate(looks, axis=0) - ELEMENTS
+    lane = lax.broadcasted_iota(jnp.int32, look.shape, 1)
+    row = lax.broadcasted_iota(jnp.int32, look.shape, 0)
+    own = lane // (2 * slot) == row // (2 * beams)
+    quarter = (ELEMENTS // 2) * ((row // beams) % 2 - (lane // slot) % 2)
+    parts = []
+    for d in range(dops):
+        element = d * slot + lane % slot
+        turn = jnp.bitwise_and(element * look + quarter, 2 * ELEMENTS - 1)
+        turn = jnp.where(turn >= ELEMENTS, turn - 2 * ELEMENTS, turn)
+        value = jnp.cos(turn.astype(jnp.float32) * (math.pi / ELEMENTS))
+        parts.append(jnp.where(own, value, 0.0))
+    return jnp.concatenate(parts, axis=1)
 
 
 def adapt(rows, range_code, steer, gate_dev, bin_dev):
-    dops, rngs = rows.shape[0] - 1, rows.shape[1]
+    rngs, dops = rows.shape[0], rows.shape[1] - 1
     gates = gate_dev * rngs
-    beams = steer.shape[0] // (2 * bin_dev)
+    beams = steer.shape[1]
     vmem = pl.BlockSpec(memory_space=pltpu.VMEM)
     return pl.pallas_call(
         lambda *refs: adapt_kernel(gate_dev, bin_dev, *refs),
-        in_specs=[pl.BlockSpec(memory_space=pltpu.SMEM), vmem, vmem],
+        in_specs=[vmem, vmem, vmem],
         out_specs=vmem,
         out_shape=jax.ShapeDtypeStruct((2, bin_dev, beams, gate_dev), jnp.float32),
         scratch_shapes=[pltpu.VMEM((dops, gates + 16, LANES), jnp.float32)] * 2,
@@ -457,12 +511,9 @@
     bin_dev = train_mask.shape[0]
     dops, rngs = lax.axis_size("dop"), lax.axis_size("rng")
     rows = -(-gate_dev // 16) * 16
-    spectra = channelize(raw_samples, filter_taps, bin_dev * dops, dops, rows)
-    mask_rows = jnp.repeat(jnp.transpose(train_mask), LANES // bin_dev, axis=1)
-    mask_rows = jnp.pad(mask_rows.astype(jnp.bfloat16), ((0, rows - gate_dev), (0, 0)))
-    gathered = exchange(spectra, mask_rows, dops, rngs)
-    steer = steering_rows(steer_index, dops, elem_dev)
-    return adapt(gathered, range_code, steer, gate_dev, bin_dev)
+    spectra = channelize(raw_samples, filter_taps, train_mask, bin_dev * dops, dops, rows)
+    gathered = exchange(spectra, rngs)
+    return adapt(gathered, range_code, steer_index, gate_dev, bin_dev)
 
 
 def shards(raw_samples, filter_taps, range_code, train_mask, steer_index):

time: 42.4 us -> 39.5 us (0.932)
  local copies, waits for them, and re-layouts: 4.43 us -> 0.96 us
  Pallas kernels: 35.9 us -> 38.1 us
  other arithmetic: 1.61 us -> 0 us
    pallas_call x1, Pallas kernels: 12.3 us -> 15 us  [adapt(): pl.pallas_call(lambda *refs: adapt_kernel(gate_dev, bin_dev, *refs), in_s...]
    broadcast_in_dim x3 -> x0, local copies, waits for them, and re-layouts: 1.44 us -> none  [the longest x2 1.35 us: channelize(): jnp.broadcast_to(taps, (TAPS, quarters, 2, LANES))]
    sub x1 -> x0, other arithmetic: 0.71 us -> none  [steering_table(): 2 * steer_rows[:, None, :] - ELEMENTS]
    transpose x1 -> x0, local copies, waits for them, and re-layouts: 0.65 us -> none  [channelize(): jnp.transpose(table, (5, 3, 4, 1, 0, 2))]
    pad x1 -> x0, local copies, waits for them, and re-layouts: 0.61 us -> none  [dual_shards(): jnp.pad(mask_rows.astype(jnp.bfloat16), ((0, rows - gate_dev), (0, 0)))]
    pallas_call x1, Pallas kernels: 14.7 us -> 14.2 us  [exchange(): pl.pallas_call(lambda *refs: exchange_kernel(dops, rngs, *refs), in_specs...]
    another operation x4 -> x0, other arithmetic: 0.49 us -> none
where the time goes in v2:
time: 39.5 us; the launch traced here: 39.1 us
  Pallas kernels  38.1 us (96%)
  local copies, waits for them, and re-layouts  0.96 us (2%)
    pallas_call x1, Pallas kernels, adapt(): pl.pallas_call(lambda *refs: adapt_kernel(gate_dev, bin_dev, *refs), in_s...  15 us
    pallas_call x1, Pallas kernels, exchange(): pl.pallas_call(lambda *refs: exchange_kernel(dops, rngs, *refs), in_specs...  14.2 us
    pallas_call x1, Pallas kernels, channelize(): pl.pallas_call(channelize_kernel, grid=(gates // block,), in_specs=[pl.Bl...  8.85 us
    unnamed x6, local copies, waits for them, and re-layouts  0.96 us

profile of v2, /device:TPU:0, one launch (start us, length us, event | category | flops | bytes accessed | tf_op | source)
XLA Modules:
  0.0 39.1 jit_solution(528823895818382120)
XLA Ops:
  0.0 0.0 copy-start.2
  0.0 0.0 copy-start.1
  0.0 8.9 %shard_map.64.refs_0_ = bf16[9,32,128]{2,1,0:T(8,128)(2,1)} custom-call(bf16[32,24,64,128]{3,2,1,0:T(8,128)(2,1)} %bitcast.5, f32[8,512]{1,0:T(8,128)} %taps_ref.1, bf16[32,1024]{1,0:T(8,128)(2,1)} %constant.2.clone.table_ref, s32[2,24]{1,0:T(2,128)} %mask_ref.1), custom_call_target="tpu_custom_call" | custom-call | tf_op jit(solution)/shard_map/pallas_call | solution.py:237
  8.9 14.2 %shard_map.65.refs_2_ = bf16[4,9,32,128]{3,2,1,0:T(8,128)(2,1)} custom-call(bf16[9,32,128]{2,1,0:T(8,128)(2,1)} %shard_map.64.refs_0_), custom_call_target="tpu_custom_call" | custom-call | tf_op jit(solution)/shard_map/pallas_call | solution.py:306
  23.0 0.0 copy-done.2
  23.1 0.0 copy-done.1
  23.1 0.0 copy-start
  23.1 1.0 %copy-done = bf16[4,9,32,128]{3,2,1,0:T(8,128)(2,1)S(1)} copy-done((bf16[4,9,32,128]{3,2,1,0:T(8,128)(2,1)S(1)}, bf16[4,9,32,128]{3,2,1,0:T(8,128)(2,1)}, u32[]{:S(2)}) %copy-start) | copy-done | bytes 294936
  24.0 15.0 %shard_map.66 = f32[2,2,4,24]{3,2,1,0:T(4,128)} custom-call(f32[2,7]{1,0:T(2,128)S(1)} %copy-done.1, s32[2,4]{1,0:T(2,128)S(1)} %copy-done.2, bf16[4,9,32,128]{3,2,1,0:T(8,128)(2,1)S(1)} %copy-done), custom_call_target="tpu_custom_call" | custom-call | tf_op jit(solution)/shard_map/pallas_call | solution.py:499
Async XLA Ops:
  0.0 23.1 %copy-start.2 = (s32[2,4]{1,0:T(2,128)S(1)}, s32[2,4]{1,0:T(2,128)}, u32[]{:S(2)}) copy-start(s32[2,4]{1,0:T(2,128)} %refs_1_.1) | copy-start | bytes 100
  0.0 23.1 %copy-start.1 = (f32[2,7]{1,0:T(2,128)S(1)}, f32[2,7]{1,0:T(2,128)}, u32[]{:S(2)}) copy-start(f32[2,7]{1,0:T(2,128)} %refs_0_.1) | copy-start | bytes 172
  23.1 1.0 %copy-start = (bf16[4,9,32,128]{3,2,1,0:T(8,128)(2,1)S(1)}, bf16[4,9,32,128]{3,2,1,0:T(8,128)(2,1)}, u32[]{:S(2)}) copy-start(bf16[4,9,32,128]{3,2,1,0:T(8,128)(2,1)} %shard_map.65.refs_2_) | copy-start | bytes 884740

commit v3 on v2

--- a/solution.py
+++ b/solution.py
@@ -177,9 +177,10 @@
     parts = [
         filt_ref[pl.ds(i, gates * elems, stride=8), :].astype(jnp.bfloat16) for i in range(8)
     ]
-    chunk = lax.dot_general(
-        table_ref[...], jnp.concatenate(parts, axis=1), NT, preferred_element_type=jnp.float32
-    )
+    chunk = jnp.dot(
+        jnp.concatenate(parts, axis=1), table_ref[...], preferred_element_type=jnp.float32
+    )
+    chunk = jnp.transpose(chunk)
     lane = lax.broadcasted_iota(jnp.int32, (dops, LANES), 1)
     for q in range(gates):
         row = jnp.zeros((dops, LANES), jnp.float32)
@@ -231,7 +232,10 @@
     view = jnp.transpose(view, (0, 1, 3, 2, 4)).reshape(elems, gates, 2 * TAPS * quarters, LANES)
     table = constant_table(bin_total).reshape(2, quarters, LANES, 2, dops, bin_dev)
     table = jnp.asarray(
-        np.transpose(table, (5, 3, 4, 1, 0, 2)).reshape(2 * bin_total, 2 * CHANNELS)
+        np.pad(
+            np.transpose(table, (1, 0, 2, 5, 3, 4)).reshape(2 * CHANNELS, 2 * bin_total),
+            ((0, 0), (0, LANES - 2 * bin_total)),
+        )
     )
     block = LANES // elems
     return pl.pallas_call(
@@ -314,7 +318,9 @@
             pltpu.SemaphoreType.DMA((rngs,)),
             pltpu.SemaphoreType.DMA((rngs,)),
         ],
-        compiler_params=pltpu.CompilerParams(collective_id=0, has_side_effects=True),
+        compiler_params=pltpu.CompilerParams(
+            collective_id=0, has_side_effects=True, vmem_limit_bytes=8 * 1024 * 1024
+        ),
     )(spectra)
 
 
@@ -369,6 +375,7 @@
     slot = LANES // (2 * bin_dev)
     lane_dev = lax.broadcasted_iota(jnp.int32, (gate_dev, LANES), 1)
     lane = lax.broadcasted_iota(jnp.int32, (gates, LANES), 1)
+    chosen = lax.rem(lax.axis_index("rng"), bin_dev)
     mask = jnp.concatenate(
         [rows_ref[r, dops].astype(jnp.float32)[:gate_dev] for r in range(rngs)], axis=0
     )
@@ -401,25 +408,19 @@
     def dot(a, b):
         return lax.dot_general(a, b, NT, preferred_element_type=jnp.float32)
 
-    def of_bins(parts):
-        rows = []
-        for k in range(bin_dev):
-            own = lane // (2 * slot) == k
-            rows.append(
-                jnp.concatenate(
-                    [jnp.where(own, x.astype(jnp.float32), 0.0).astype(jnp.bfloat16) for x in parts],
-                    axis=1,
-                )
-            )
-        return jnp.concatenate(rows, axis=0)
-
-    signal_bins, train_bins = of_bins(signal), of_bins(train)
+    own = lane // (2 * slot) == chosen
+
+    def of_bin(parts):
+        kept = [jnp.where(own, x.astype(jnp.float32), 0.0).astype(jnp.bfloat16) for x in parts]
+        return jnp.concatenate(kept, axis=1)
+
+    signal_bins, train_bins = of_bin(signal), of_bin(train)
     signal, turned, train, train_turned = (
         jnp.concatenate(x, axis=1) for x in (signal, turned, train, train_turned)
     )
     all_re, all_im = dot(signal_bins, signal), dot(signal_bins, turned)
     gram_re, gram_im = dot(train_bins, train), dot(train_bins, train_turned)
-    steer = steering_rows(steer_ref[...], dops, slot)
+    steer = steering_rows(steer_ref[...], chosen, dops, slot)
     high = steer.astype(jnp.bfloat16)
     rest = steer - high.astype(jnp.float32)
     middle = rest.astype(jnp.bfloat16)
@@ -427,60 +428,92 @@
     looks = dot(high, signal) + (dot(middle, signal) + dot(low, signal))
     sights = dot(high, train) + (dot(middle, train) + dot(low, train))
     norms = jnp.sum(steer * steer, axis=1, keepdims=True)
-    beams = steer.shape[0] // (2 * bin_dev)
+    beams = steer.shape[0] // 2
     diagonal = (
         lax.broadcasted_iota(jnp.int32, (gates, gates), 0)
         == lax.broadcasted_iota(jnp.int32, (gates, gates), 1)
     )
     loading = jnp.where(diagonal, loading_level * gates, 0.0)
-    problems = []
-    for k in range(bin_dev):
-        at, b = k * gates, 2 * k * beams
-        problems.append(
-            (
-                gram_re[at : at + gates] + loading,
-                -gram_im[at : at + gates],
-                sights[b : b + beams],
-                sights[b + beams : b + 2 * beams],
-            )
-        )
-    solved = eliminate(problems)
-    place = lax.axis_index("rng")
+    b_re, b_im = sights[:beams], sights[beams:]
+    y_re, y_im = eliminate([(gram_re + loading, -gram_im, b_re, b_im)])[0]
     highest = lax.Precision.HIGHEST
-    for k in range(bin_dev):
-        y_re, y_im = solved[k]
-        b_re, b_im = problems[k][2:]
-        at, b = k * gates, 2 * k * beams
-        k_re, k_im = all_re[at : at + gates], all_im[at : at + gates]
-        both = jnp.concatenate([y_re, y_im], axis=0)
-        by_re = jnp.dot(both, k_re, precision=highest, preferred_element_type=jnp.float32)
-        by_im = jnp.dot(both, k_im, precision=highest, preferred_element_type=jnp.float32)
-        o_re = looks[b : b + beams] - (by_re[:beams] + by_im[beams:])
-        o_im = looks[b + beams : b + 2 * beams] - (by_re[beams:] - by_im[:beams])
-        lost = jnp.sum(b_re * y_re + b_im * y_im, axis=1, keepdims=True)
-        response = (norms[b : b + beams] - lost) / loading_level
-        scale = 1.0 / (loading_level * jnp.sqrt(response))
-        for part, o in enumerate((o_re, o_im)):
-            o = o * scale
-            mine = o[:, :gate_dev]
-            for r in range(1, rngs):
-                mine = jnp.where(place == r, o[:, r * gate_dev : (r + 1) * gate_dev], mine)
-            out_ref[part, k] = mine
-
-
-def steering_rows(steer_index, dops, slot):
+    both = jnp.concatenate([y_re, y_im], axis=0)
+    by_re = jnp.dot(both, all_re, precision=highest, preferred_element_type=jnp.float32)
+    by_im = jnp.dot(both, all_im, precision=highest, preferred_element_type=jnp.float32)
+    o_re = looks[:beams] - (by_re[:beams] + by_im[beams:])
+    o_im = looks[beams:] - (by_re[beams:] - by_im[:beams])
+    lost = jnp.sum(b_re * y_re + b_im * y_im, axis=1, keepdims=True)
+    response = (norms[:beams] - lost) / loading_level
+    scale = 1.0 / (loading_level * jnp.sqrt(response))
+    out = jnp.concatenate([o_re * scale, o_im * scale], axis=0)
+    if gates < LANES:
+        out = jnp.concatenate(
+            [out, jnp.zeros((2 * beams, LANES - gates), jnp.float32)], axis=1
+        )
+    out_ref[...] = out
+
+
+def swap_kernel(gate_dev, rngs, mine_ref, out_ref, other_ref, send, recv):
+    d, r = lax.axis_index("dop"), lax.axis_index("rng")
+    chosen = lax.rem(r, 2)
+    partner = (d, r + 1 - 2 * chosen)
+    barrier = pltpu.get_barrier_semaphore()
+    pl.semaphore_signal(barrier, inc=1, device_id=partner, device_id_type=MESH)
+    pl.semaphore_wait(barrier, 1)
+    copy = pltpu.make_async_remote_copy(
+        src_ref=mine_ref,
+        dst_ref=other_ref,
+        send_sem=send,
+        recv_sem=recv,
+        device_id=partner,
+        device_id_type=MESH,
+    )
+    copy.start()
+    copy.wait()
+    beams = mine_ref.shape[0] // 2
+
+    def own_gates(x):
+        out = x[:, :gate_dev]
+        for i in range(1, rngs):
+            out = jnp.where(r == i, x[:, i * gate_dev : (i + 1) * gate_dev], out)
+        return out
+
+    mine, other = own_gates(mine_ref[...]), own_gates(other_ref[...])
+    for k in range(2):
+        both = jnp.where(chosen == k, mine, other)
+        for part in range(2):
+            out_ref[part, k] = both[part * beams : (part + 1) * beams]
+
+
+def swap(mine, gate_dev, rngs):
+    vmem = pl.BlockSpec(memory_space=pltpu.VMEM)
+    return pl.pallas_call(
+        lambda *refs: swap_kernel(gate_dev, rngs, *refs),
+        in_specs=[vmem],
+        out_specs=vmem,
+        out_shape=jax.ShapeDtypeStruct((2, 2, mine.shape[0] // 2, gate_dev), jnp.float32),
+        scratch_shapes=[
+            pltpu.VMEM(mine.shape, jnp.float32),
+            pltpu.SemaphoreType.DMA,
+            pltpu.SemaphoreType.DMA,
+        ],
+        compiler_params=pltpu.CompilerParams(
+            collective_id=1, has_side_effects=True, vmem_limit_bytes=8 * 1024 * 1024
+        ),
+    )(mine)
+
+
+def steering_rows(steer_index, chosen, dops, slot):
     bins, beams = steer_index.shape
-    looks = [
-        jnp.broadcast_to(steer_index[k : k + 1, j : j + 1], (1, LANES))
-        for k in range(bins)
-        for _ in range(2)
-        for j in range(beams)
-    ]
-    look = 2 * jnp.concatenate(looks, axis=0) - ELEMENTS
+    picked = steer_index[:1]
+    for k in range(1, bins):
+        picked = jnp.where(chosen == k, steer_index[k : k + 1], picked)
+    looks = [jnp.broadcast_to(picked[:, j : j + 1], (1, LANES)) for j in range(beams)]
+    look = 2 * jnp.concatenate(looks + looks, axis=0) - ELEMENTS
     lane = lax.broadcasted_iota(jnp.int32, look.shape, 1)
     row = lax.broadcasted_iota(jnp.int32, look.shape, 0)
-    own = lane // (2 * slot) == row // (2 * beams)
-    quarter = (ELEMENTS // 2) * ((row // beams) % 2 - (lane // slot) % 2)
+    own = lane // (2 * slot) == chosen
+    quarter = (ELEMENTS // 2) * (row // beams - (lane // slot) % 2)
     parts = []
     for d in range(dops):
         element = d * slot + lane % slot
@@ -500,7 +533,7 @@
         lambda *refs: adapt_kernel(gate_dev, bin_dev, *refs),
         in_specs=[vmem, vmem, vmem],
         out_specs=vmem,
-        out_shape=jax.ShapeDtypeStruct((2, bin_dev, beams, gate_dev), jnp.float32),
+        out_shape=jax.ShapeDtypeStruct((2 * beams, LANES), jnp.float32),
         scratch_shapes=[pltpu.VMEM((dops, gates + 16, LANES), jnp.float32)] * 2,
         compiler_params=pltpu.CompilerParams(vmem_limit_bytes=32 * 1024 * 1024),
     )(range_code, steer, rows)
@@ -513,7 +546,8 @@
     rows = -(-gate_dev // 16) * 16
     spectra = channelize(raw_samples, filter_taps, train_mask, bin_dev * dops, dops, rows)
     gathered = exchange(spectra, rngs)
-    return adapt(gathered, range_code, steer_index, gate_dev, bin_dev)
+    mine = adapt(gathered, range_code, steer_index, gate_dev, bin_dev)
+    return swap(mine, gate_dev, rngs)
 
 
 def shards(raw_samples, filter_taps, range_code, train_mask, steer_index):
@@ -522,6 +556,8 @@
     fits = (
         2 * train_mask.shape[0] * elem_dev == LANES
         and dops == 8
+        and train_mask.shape[0] == 2
+        and rngs % 2 == 0
         and gate_dev % 8 == 0
         and gate_dev * rngs <= LANES
     )

time: 39.5 us -> 38.3 us (0.970)
  Pallas kernels: 38.1 us -> 36.5 us
  local copies, waits for them, and re-layouts: 0.96 us -> 1.49 us
    pallas_call x1, Pallas kernels: 15 us -> 12.9 us  [adapt(): pl.pallas_call(lambda *refs: adapt_kernel(gate_dev, bin_dev, *refs), in_s...]
    pallas_call x0 -> x1, Pallas kernels: none -> 1.75 us  [swap(): pl.pallas_call(lambda *refs: swap_kernel(gate_dev, rngs, *refs), in_specs...]
    pallas_call x1, Pallas kernels: 14.2 us -> 12.6 us  [exchange(): pl.pallas_call(lambda *refs: exchange_kernel(dops, rngs, *refs), in_specs...]
    unnamed x6 -> x7, local copies, waits for them, and re-layouts: 0.96 us -> 1.49 us
    pallas_call x1, Pallas kernels: 8.85 us -> 9.25 us  [channelize(): pl.pallas_call(channelize_kernel, grid=(gates // block,), in_specs=[pl.Bl...]
where the time goes in v3:
time: 38.3 us; the launch traced here: 38 us
  Pallas kernels  36.5 us (95%)
  local copies, waits for them, and re-layouts  1.49 us (4%)
    pallas_call x1, Pallas kernels, adapt(): pl.pallas_call(lambda *refs: adapt_kernel(gate_dev, bin_dev, *refs), in_s...  12.9 us
    pallas_call x1, Pallas kernels, exchange(): pl.pallas_call(lambda *refs: exchange_kernel(dops, rngs, *refs), in_specs...  12.6 us
    pallas_call x1, Pallas kernels, channelize(): pl.pallas_call(channelize_kernel, grid=(gates // block,), in_specs=[pl.Bl...  9.25 us
    pallas_call x1, Pallas kernels, swap(): pl.pallas_call(lambda *refs: swap_kernel(gate_dev, rngs, *refs), in_specs...  1.75 us
    unnamed x7, local copies, waits for them, and re-layouts  1.49 us

profile of v3, /device:TPU:0, one launch (start us, length us, event | category | flops | bytes accessed | tf_op | source)
XLA Modules:
  0.0 38.0 jit_solution(4356726336374824266)
XLA Ops:
  0.0 0.0 copy-start.2
  0.0 0.0 copy-start.1
  0.0 9.2 %shard_map.64.refs_0_ = bf16[9,32,128]{2,1,0:T(8,128)(2,1)} custom-call(bf16[32,24,64,128]{3,2,1,0:T(8,128)(2,1)} %bitcast.5, f32[8,512]{1,0:T(8,128)} %taps_ref.1, bf16[1024,128]{1,0:T(8,128)(2,1)} %constant.2.clone.table_ref, s32[2,24]{1,0:T(2,128)} %mask_ref.1), custom_call_target="tpu_custom_call" | custom-call | tf_op jit(solution)/shard_map/pallas_call | solution.py:241
  9.3 0.0 copy-start
  9.3 0.9 %copy-done = bf16[9,32,128]{2,1,0:T(8,128)(2,1)S(1)} copy-done((bf16[9,32,128]{2,1,0:T(8,128)(2,1)S(1)}, bf16[9,32,128]{2,1,0:T(8,128)(2,1)}, u32[]{:S(2)}) %copy-start) | copy-done | bytes 73752
  10.1 12.6 %shard_map.65.refs_2_ = bf16[4,9,32,128]{3,2,1,0:T(8,128)(2,1)S(1)} custom-call(bf16[9,32,128]{2,1,0:T(8,128)(2,1)S(1)} %copy-done), custom_call_target="tpu_custom_call" | custom-call | tf_op jit(solution)/shard_map/pallas_call | solution.py:310
  22.7 0.0 copy-done.2
  22.8 0.0 copy-done.1
  22.8 12.9 %shard_map.66.refs_0_ = f32[8,128]{1,0:T(8,128)S(1)} custom-call(f32[2,7]{1,0:T(2,128)S(1)} %copy-done.1, s32[2,4]{1,0:T(2,128)S(1)} %copy-done.2, bf16[4,9,32,128]{3,2,1,0:T(8,128)(2,1)S(1)} %shard_map.65.refs_2_), custom_call_target="tpu_custom_call" | custom-call | tf_op jit(solution)/shard_map/pallas_call | solution.py:532
  35.7 1.7 %shard_map.67 = f32[2,2,4,24]{3,2,1,0:T(4,128)S(1)} custom-call(f32[8,128]{1,0:T(8,128)S(1)} %shard_map.66.refs_0_), custom_call_target="tpu_custom_call" | custom-call | tf_op jit(solution)/shard_map/pallas_call | solution.py:490
  37.4 0.6 %copy.9 = f32[2,2,4,24]{3,2,1,0:T(4,128)} copy(f32[2,2,4,24]{3,2,1,0:T(4,128)S(1)} %shard_map.67) | data formatting | bytes 3072
Async XLA Ops:
  0.0 22.8 %copy-start.2 = (s32[2,4]{1,0:T(2,128)S(1)}, s32[2,4]{1,0:T(2,128)}, u32[]{:S(2)}) copy-start(s32[2,4]{1,0:T(2,128)} %refs_1_.1) | copy-start | bytes 100
  0.0 22.8 %copy-start.1 = (f32[2,7]{1,0:T(2,128)S(1)}, f32[2,7]{1,0:T(2,128)}, u32[]{:S(2)}) copy-start(f32[2,7]{1,0:T(2,128)} %refs_0_.1) | copy-start | bytes 172
  9.3 0.9 %copy-start = (bf16[9,32,128]{2,1,0:T(8,128)(2,1)S(1)}, bf16[9,32,128]{2,1,0:T(8,128)(2,1)}, u32[]{:S(2)}) copy-start(bf16[9,32,128]{2,1,0:T(8,128)(2,1)} %shard_map.64.refs_0_) | copy-start | bytes 221188

commit v4 on v3

--- a/solution.py
+++ b/solution.py
@@ -151,113 +151,7 @@
     return jnp.where(imag, pltpu.roll(x, slot, 1), -pltpu.roll(x, LANES - slot, 1))
 
 
-def channelize_kernel(raw_ref, taps_ref, table_ref, mask_ref, out_ref, filt_ref, spec_ref):
-    elems, gates = raw_ref.shape[0], raw_ref.shape[1]
-    dops, rows = out_ref.shape[0] - 1, out_ref.shape[1]
-    step, steps = pl.program_id(0), pl.num_programs(0)
-    taps = []
-    for t in range(TAPS):
-        quarters = [
-            jnp.broadcast_to(taps_ref[t : t + 1, i : i + LANES], (2, LANES))
-            for i in range(0, CHANNELS, LANES)
-        ]
-        taps.append(jnp.concatenate(quarters, axis=0))
-    for gate in range(gates):
-
-        def one(e, carry, gate=gate):
-            x = raw_ref[e, gate].astype(jnp.float32)
-            terms = [x[8 * t : 8 * t + 8] * taps[t] for t in range(TAPS)]
-            while len(terms) > 1:
-                terms = [a + b for a, b in zip(terms[::2], terms[1::2])]
-            at = pl.multiple_of((gate * elems + e) * 8, 8)
-            filt_ref[pl.ds(at, 8), :] = terms[0]
-            return carry
-
-        lax.fori_loop(0, elems, one, 0, unroll=8)
-    parts = [
-        filt_ref[pl.ds(i, gates * elems, stride=8), :].astype(jnp.bfloat16) for i in range(8)
-    ]
-    chunk = jnp.dot(
-        jnp.concatenate(parts, axis=1), table_ref[...], preferred_element_type=jnp.float32
-    )
-    chunk = jnp.transpose(chunk)
-    lane = lax.broadcasted_iota(jnp.int32, (dops, LANES), 1)
-    for q in range(gates):
-        row = jnp.zeros((dops, LANES), jnp.float32)
-        for c in range(LANES // elems):
-            piece = chunk[c * dops : (c + 1) * dops]
-            shift = ((c - q) * elems) % LANES
-            if shift:
-                piece = pltpu.roll(piece, shift, 1)
-            row = jnp.where(lane // elems == c, piece, row)
-        at = pl.multiple_of((step * gates + q) * dops, 8)
-        spec_ref[pl.ds(at, dops), :] = row
-
-    @pl.when(step == steps - 1)
-    def _():
-        full = steps * gates
-        if rows > full:
-            spec_ref[pl.ds(full * dops, (rows - full) * dops), :] = jnp.zeros(
-                ((rows - full) * dops, LANES), jnp.float32
-            )
-        for d in range(dops):
-            out_ref[d] = spec_ref[pl.ds(d, rows, stride=dops), :].astype(jnp.bfloat16)
-        bins, own = mask_ref.shape
-        held = mask_ref[...].astype(jnp.float32)
-        lane = lax.broadcasted_iota(jnp.int32, (bins, LANES), 1)
-        bin_row = lax.broadcasted_iota(jnp.int32, (bins, LANES), 0)
-        spread = jnp.where(lane // (LANES // bins) == bin_row, 1.0, 0.0)
-        column = lax.dot_general(
-            held, spread, (((0,), (0,)), ((), ())), preferred_element_type=jnp.float32
-        )
-        column = jnp.concatenate([column, jnp.zeros((rows - own, LANES), jnp.float32)], axis=0)
-        out_ref[dops] = column.astype(jnp.bfloat16)
-
-
-def constant_table(bin_total):
-    mode_index, bin_index = np.arange(CHANNELS), np.arange(bin_total)
-    turn_count = np.mod(mode_index[:, None] * bin_index[None, :], CHANNELS).astype(np.float32)
-    phases = turn_count * np.float32(2.0 * math.pi / CHANNELS)
-    cosine = np.cos(phases) / np.float32(math.sqrt(CHANNELS))
-    sine_part = np.sin(phases) / np.float32(math.sqrt(CHANNELS))
-    table = np.block([[cosine, -sine_part], [sine_part, cosine]])
-    return table.astype(ml_dtypes.bfloat16)
-
-
-def channelize(raw, filter_taps, train_mask, bin_total, dops, rows):
-    elems, gates = raw.shape[0], raw.shape[1]
-    bin_dev = bin_total // dops
-    quarters = CHANNELS // LANES
-    view = raw.reshape(elems, gates, 2, TAPS * quarters, LANES)
-    view = jnp.transpose(view, (0, 1, 3, 2, 4)).reshape(elems, gates, 2 * TAPS * quarters, LANES)
-    table = constant_table(bin_total).reshape(2, quarters, LANES, 2, dops, bin_dev)
-    table = jnp.asarray(
-        np.pad(
-            np.transpose(table, (1, 0, 2, 5, 3, 4)).reshape(2 * CHANNELS, 2 * bin_total),
-            ((0, 0), (0, LANES - 2 * bin_total)),
-        )
-    )
-    block = LANES // elems
-    return pl.pallas_call(
-        channelize_kernel,
-        grid=(gates // block,),
-        in_specs=[
-            pl.BlockSpec((elems, block, 2 * TAPS * quarters, LANES), lambda i: (0, i, 0, 0)),
-            pl.BlockSpec(filter_taps.shape, lambda i: (0, 0)),
-            pl.BlockSpec(table.shape, lambda i: (0, 0)),
-            pl.BlockSpec(train_mask.shape, lambda i: (0, 0)),
-        ],
-        out_specs=pl.BlockSpec((dops + 1, rows, LANES), lambda i: (0, 0, 0)),
-        out_shape=jax.ShapeDtypeStruct((dops + 1, rows, LANES), jnp.bfloat16),
-        scratch_shapes=[
-            pltpu.VMEM((elems * block * 8, LANES), jnp.float32),
-            pltpu.VMEM((rows * dops, LANES), jnp.float32),
-        ],
-        compiler_params=pltpu.CompilerParams(vmem_limit_bytes=56 * 1024 * 1024),
-    )(view, filter_taps, table, train_mask)
-
-
-def exchange_kernel(dops, rngs, spec_ref, out_ref, send1, recv1, send2, recv2):
+def greet(dops, rngs):
     d, r = lax.axis_index("dop"), lax.axis_index("rng")
     barrier = pltpu.get_barrier_semaphore()
     for i in range(1, dops):
@@ -268,7 +162,11 @@
         pl.semaphore_signal(
             barrier, inc=1, device_id=(d, lax.rem(r + j, rngs)), device_id_type=MESH
         )
-    pl.semaphore_wait(barrier, dops + rngs - 2)
+
+
+def exchange(dops, rngs, spec_ref, out_ref, send1, recv1, send2, recv2):
+    d, r = lax.axis_index("dop"), lax.axis_index("rng")
+    pl.semaphore_wait(pltpu.get_barrier_semaphore(), dops + rngs - 2)
     turns = []
     for i in range(1, dops):
         to = lax.rem(d + i, dops)
@@ -305,68 +203,165 @@
         copy.wait_send()
 
 
-def exchange(spectra, rngs):
-    dops = spectra.shape[0] - 1
+def gather_kernel(
+    raw_ref, taps_ref, table_ref, mask_ref, out_ref, filt_ref, spec_ref, own_ref, all_ref, *semaphores
+):
+    elems, gates = raw_ref.shape[0], raw_ref.shape[1]
+    rngs, dops, rows = out_ref.shape[0], out_ref.shape[1] - 1, out_ref.shape[2]
+    step, steps = pl.program_id(0), pl.num_programs(0)
+
+    @pl.when(step == 0)
+    def _():
+        greet(dops, rngs)
+
+    taps = []
+    for t in range(TAPS):
+        quarters = [
+            jnp.broadcast_to(taps_ref[t : t + 1, i : i + LANES], (2, LANES))
+            for i in range(0, CHANNELS, LANES)
+        ]
+        taps.append(jnp.concatenate(quarters, axis=0))
+    for gate in range(gates):
+
+        def one(e, carry, gate=gate):
+            x = raw_ref[e, gate].astype(jnp.float32)
+            terms = [x[8 * t : 8 * t + 8] * taps[t] for t in range(TAPS)]
+            while len(terms) > 1:
+                terms = [a + b for a, b in zip(terms[::2], terms[1::2])]
+            at = pl.multiple_of((gate * elems + e) * 8, 8)
+            filt_ref[pl.ds(at, 8), :] = terms[0]
+            return carry
+
+        lax.fori_loop(0, elems, one, 0, unroll=8)
+    parts = [
+        filt_ref[pl.ds(i, gates * elems, stride=8), :].astype(jnp.bfloat16) for i in range(8)
+    ]
+    chunk = lax.dot_general(
+        table_ref[...], jnp.concatenate(parts, axis=1), NT, preferred_element_type=jnp.float32
+    )
+    lane = lax.broadcasted_iota(jnp.int32, (dops, LANES), 1)
+    for q in range(gates):
+        row = jnp.zeros((dops, LANES), jnp.float32)
+        for c in range(LANES // elems):
+            piece = chunk[c * dops : (c + 1) * dops]
+            shift = ((c - q) * elems) % LANES
+            if shift:
+                piece = pltpu.roll(piece, shift, 1)
+            row = jnp.where(lane // elems == c, piece, row)
+        at = pl.multiple_of((step * gates + q) * dops, 8)
+        spec_ref[pl.ds(at, dops), :] = row
+
+    @pl.when(step == steps - 1)
+    def _():
+        full = steps * gates
+        if rows > full:
+            spec_ref[pl.ds(full * dops, (rows - full) * dops), :] = jnp.zeros(
+                ((rows - full) * dops, LANES), jnp.float32
+            )
+        for d in range(dops):
+            own_ref[d] = spec_ref[pl.ds(d, rows, stride=dops), :].astype(jnp.bfloat16)
+        bins, own = mask_ref.shape
+        held = mask_ref[...].astype(jnp.float32)
+        lane = lax.broadcasted_iota(jnp.int32, (bins, LANES), 1)
+        bin_row = lax.broadcasted_iota(jnp.int32, (bins, LANES), 0)
+        spread = jnp.where(lane // (LANES // bins) == bin_row, 1.0, 0.0)
+        column = lax.dot_general(
+            held, spread, (((0,), (0,)), ((), ())), preferred_element_type=jnp.float32
+        )
+        column = jnp.concatenate([column, jnp.zeros((rows - own, LANES), jnp.float32)], axis=0)
+        own_ref[dops] = column.astype(jnp.bfloat16)
+        exchange(dops, rngs, own_ref, all_ref, *semaphores)
+        out_ref[...] = all_ref[...]
+
+
+def constant_table(bin_total):
+    mode_index, bin_index = np.arange(CHANNELS), np.arange(bin_total)
+    turn_count = np.mod(mode_index[:, None] * bin_index[None, :], CHANNELS).astype(np.float32)
+    phases = turn_count * np.float32(2.0 * math.pi / CHANNELS)
+    cosine = np.cos(phases) / np.float32(math.sqrt(CHANNELS))
+    sine_part = np.sin(phases) / np.float32(math.sqrt(CHANNELS))
+    table = np.block([[cosine, -sine_part], [sine_part, cosine]])
+    return table.astype(ml_dtypes.bfloat16)
+
+
+def gather(raw, filter_taps, train_mask, bin_total, dops, rngs, rows):
+    elems, gates = raw.shape[0], raw.shape[1]
+    bin_dev = bin_total // dops
+    quarters = CHANNELS // LANES
+    view = raw.reshape(elems, gates, 2, TAPS * quarters, LANES)
+    view = jnp.transpose(view, (0, 1, 3, 2, 4)).reshape(elems, gates, 2 * TAPS * quarters, LANES)
+    table = constant_table(bin_total).reshape(2, quarters, LANES, 2, dops, bin_dev)
+    table = jnp.asarray(
+        np.transpose(table, (5, 3, 4, 1, 0, 2)).reshape(2 * bin_total, 2 * CHANNELS)
+    )
+    block = LANES // elems
     return pl.pallas_call(
-        lambda *refs: exchange_kernel(dops, rngs, *refs),
-        in_specs=[pl.BlockSpec(memory_space=pltpu.VMEM)],
+        gather_kernel,
+        grid=(gates // block,),
+        in_specs=[
+            pl.BlockSpec((elems, block, 2 * TAPS * quarters, LANES), lambda i: (0, i, 0, 0)),
+            pl.BlockSpec(filter_taps.shape, lambda i: (0, 0)),
+            pl.BlockSpec(table.shape, lambda i: (0, 0)),
+            pl.BlockSpec(train_mask.shape, lambda i: (0, 0)),
+        ],
         out_specs=pl.BlockSpec(memory_space=pltpu.VMEM),
-        out_shape=jax.ShapeDtypeStruct((rngs,) + spectra.shape, jnp.bfloat16),
+        out_shape=jax.ShapeDtypeStruct((rngs, dops + 1, rows, LANES), jnp.bfloat16),
         scratch_shapes=[
+            pltpu.VMEM((elems * block * 8, LANES), jnp.float32),
+            pltpu.VMEM((rows * dops, LANES), jnp.float32),
+            pltpu.VMEM((dops + 1, rows, LANES), jnp.bfloat16),
+            pltpu.VMEM((rngs, dops + 1, rows, LANES), jnp.bfloat16),
             pltpu.SemaphoreType.DMA((dops,)),
             pltpu.SemaphoreType.DMA((dops,)),
             pltpu.SemaphoreType.DMA((rngs,)),
             pltpu.SemaphoreType.DMA((rngs,)),
         ],
         compiler_params=pltpu.CompilerParams(
-            collective_id=0, has_side_effects=True, vmem_limit_bytes=8 * 1024 * 1024
+            collective_id=0, has_side_effects=True, vmem_limit_bytes=53 * 1024 * 1024
         ),
-    )(spectra)
-
-
-def eliminate(problems):
-    states = []
-    for a_re, a_im, b_re, b_im in problems:
-        size = a_re.shape[0]
-        tiles = [
-            [a_re[i : i + 8], a_im[i : i + 8]] for i in range(0, size, 8)
-        ] + [[b_re, b_im]]
-        states.append(tiles)
-    lanes = {
-        rows: lax.broadcasted_iota(jnp.int32, (rows, size), 1) for rows in (1, 8, b_re.shape[0])
-    }
+    )(view, filter_taps, table, train_mask)
+
+
+def eliminate(a_re, a_im, b_re, b_im):
+    size = a_re.shape[0]
+    tiles = [[a_re[i : i + 8], a_im[i : i + 8]] for i in range(0, size, 8)] + [[b_re, b_im]]
+    shape = (8, size)
+    lane = lax.broadcasted_iota(jnp.int32, shape, 1)
     for p in range(0, size, 2):
         first, s = divmod(p, 8)
-        for tiles in states:
-            u_re, u_im = (part[s : s + 1] for part in tiles[first])
-            v_re, v_im = (part[s + 1 : s + 2] for part in tiles[first])
-            a, c = u_re[:, p : p + 1], v_re[:, p + 1 : p + 2]
-            b_re, b_im = u_re[:, p + 1 : p + 2], u_im[:, p + 1 : p + 2]
-            inverse = 1.0 / (a * c - (b_re * b_re + b_im * b_im))
-            a, c, b_re, b_im = a * inverse, c * inverse, b_re * inverse, b_im * inverse
-            one, two = lanes[1] == p, lanes[1] == p + 1
-            pair = one | two
-            u_re = jnp.where(pair, jnp.where(one, -1.0, 0.0), u_re)
-            v_re = jnp.where(pair, jnp.where(two, -1.0, 0.0), v_re)
-            u_im, v_im = jnp.where(pair, 0.0, u_im), jnp.where(pair, 0.0, v_im)
-            f_re = c * u_re - (b_re * v_re - b_im * v_im)
-            f_im = c * u_im - (b_re * v_im + b_im * v_re)
-            g_re = a * v_re - (b_re * u_re + b_im * u_im)
-            g_im = a * v_im - (b_re * u_im - b_im * u_re)
-            begin = first + 1 if s == 6 else first
-            for tile in tiles[begin:]:
-                t_re, t_im = tile
-                x_re, x_im = t_re[:, p : p + 1], t_im[:, p : p + 1]
-                y_re, y_im = t_re[:, p + 1 : p + 2], t_im[:, p + 1 : p + 2]
-                at = lanes[t_re.shape[0]]
-                keep = (at != p) & (at != p + 1)
-                tile[0] = jnp.where(keep, t_re, 0.0) - (
-                    (x_re * f_re - x_im * f_im) + (y_re * g_re - y_im * g_im)
-                )
-                tile[1] = jnp.where(keep, t_im, 0.0) - (
-                    (x_re * f_im + x_im * f_re) + (y_re * g_im + y_im * g_re)
-                )
-    return [tiles[-1] for tiles in states]
+
+        def row(part, i):
+            return jnp.broadcast_to(part[i : i + 1], shape)
+
+        def column(part, i):
+            return jnp.broadcast_to(part[:, i : i + 1], shape)
+
+        u_re, u_im = (row(part, s) for part in tiles[first])
+        v_re, v_im = (row(part, s + 1) for part in tiles[first])
+        a, c = column(u_re, p), column(v_re, p + 1)
+        b_re, b_im = column(u_re, p + 1), column(u_im, p + 1)
+        inverse = 1.0 / (a * c - (b_re * b_re + b_im * b_im))
+        one, two = lane == p, lane == p + 1
+        pair = one | two
+        u_re = jnp.where(pair, jnp.where(one, -1.0, 0.0), u_re)
+        v_re = jnp.where(pair, jnp.where(two, -1.0, 0.0), v_re)
+        u_im, v_im = jnp.where(pair, 0.0, u_im), jnp.where(pair, 0.0, v_im)
+        f_re = (c * u_re - (b_re * v_re - b_im * v_im)) * inverse
+        f_im = (c * u_im - (b_re * v_im + b_im * v_re)) * inverse
+        g_re = (a * v_re - (b_re * u_re + b_im * u_im)) * inverse
+        g_im = (a * v_im - (b_re * u_im - b_im * u_re)) * inverse
+        begin = first + 1 if s == 6 else first
+        for tile in tiles[begin:]:
+            t_re, t_im = tile
+            x_re, x_im = column(t_re, p), column(t_im, p)
+            y_re, y_im = column(t_re, p + 1), column(t_im, p + 1)
+            tile[0] = jnp.where(pair, 0.0, t_re) - (
+                (x_re * f_re - x_im * f_im) + (y_re * g_re - y_im * g_im)
+            )
+            tile[1] = jnp.where(pair, 0.0, t_im) - (
+                (x_re * f_im + x_im * f_re) + (y_re * g_im + y_im * g_re)
+            )
+    return tiles[-1]
 
 
 def adapt_kernel(gate_dev, bin_dev, code_ref, steer_ref, rows_ref, out_ref, self_ref, turned_ref):
@@ -435,7 +430,9 @@
     )
     loading = jnp.where(diagonal, loading_level * gates, 0.0)
     b_re, b_im = sights[:beams], sights[beams:]
-    y_re, y_im = eliminate([(gram_re + loading, -gram_im, b_re, b_im)])[0]
+    spare = jnp.zeros((8 - beams, gates), jnp.float32)
+    sides = [jnp.concatenate([x, spare], axis=0) for x in (b_re, b_im)]
+    y_re, y_im = (x[:beams] for x in eliminate(gram_re + loading, -gram_im, *sides))
     highest = lax.Precision.HIGHEST
     both = jnp.concatenate([y_re, y_im], axis=0)
     by_re = jnp.dot(both, all_re, precision=highest, preferred_element_type=jnp.float32)
@@ -503,6 +500,21 @@
     )(mine)
 
 
+def cosine_of_turn(turn):
+    right = ELEMENTS // 2
+    quadrant = (turn + right // 2) // right
+    x = (turn - quadrant * right).astype(jnp.float32) * (math.pi / ELEMENTS)
+    z = x * x
+    sine_part = x + x * z * (-1.6666654611e-1 + z * (8.3321608736e-3 - z * 1.9515295891e-4))
+    cosine = 1.0 - 0.5 * z + z * z * (
+        4.166664568298827e-2 + z * (-1.388731625493765e-3 + z * 2.443315711809948e-5)
+    )
+    odd = jnp.bitwise_and(quadrant, 1) == 1
+    value = jnp.where(odd, sine_part, cosine)
+    flip = (quadrant == 1) | (quadrant == 2)
+    return jnp.where(flip, -value, value)
+
+
 def steering_rows(steer_index, chosen, dops, slot):
     bins, beams = steer_index.shape
     picked = steer_index[:1]
@@ -518,9 +530,7 @@
     for d in range(dops):
         element = d * slot + lane % slot
         turn = jnp.bitwise_and(element * look + quarter, 2 * ELEMENTS - 1)
-        turn = jnp.where(turn >= ELEMENTS, turn - 2 * ELEMENTS, turn)
-        value = jnp.cos(turn.astype(jnp.float32) * (math.pi / ELEMENTS))
-        parts.append(jnp.where(own, value, 0.0))
+        parts.append(jnp.where(own, cosine_of_turn(turn), 0.0))
     return jnp.concatenate(parts, axis=1)
 
 
@@ -544,8 +554,8 @@
     bin_dev = train_mask.shape[0]
     dops, rngs = lax.axis_size("dop"), lax.axis_size("rng")
     rows = -(-gate_dev // 16) * 16
-    spectra = channelize(raw_samples, filter_taps, train_mask, bin_dev * dops, dops, rows)
-    gathered = exchange(spectra, rngs)
+    total = bin_dev * dops
+    gathered = gather(raw_samples, filter_taps, train_mask, total, dops, rngs, rows)
     mine = adapt(gathered, range_code, steer_index, gate_dev, bin_dev)
     return swap(mine, gate_dev, rngs)
 
@@ -558,6 +568,7 @@
         and dops == 8
         and train_mask.shape[0] == 2
         and rngs % 2 == 0
+        and steer_index.shape[1] <= 8
         and gate_dev % 8 == 0
         and gate_dev * rngs <= LANES
     )

time: 38.3 us -> 33.4 us (0.87)
  Pallas kernels: 36.5 us -> 30.2 us
  local copies, waits for them, and re-layouts: 1.49 us -> 2.86 us
    pallas_call x1, Pallas kernels: 12.9 us -> 8.49 us  [adapt(): pl.pallas_call(lambda *refs: adapt_kernel(gate_dev, bin_dev, *refs), in_s...]
    pallas_call x2 -> x1, Pallas kernels: 21.9 us -> 20 us  [gather(): pl.pallas_call(gather_kernel, grid=(gates // block,), in_specs=[pl.BlockS...]
    unnamed x7 -> x11, local copies, waits for them, and re-layouts: 1.49 us -> 2.86 us
where the time goes in v4:
time: 33.4 us; the launch traced here: 33.1 us
  Pallas kernels  30.2 us (90%)
  local copies, waits for them, and re-layouts  2.86 us (9%)
    pallas_call x1, Pallas kernels, gather(): pl.pallas_call(gather_kernel, grid=(gates // block,), in_specs=[pl.BlockS...  20 us
    pallas_call x1, Pallas kernels, adapt(): pl.pallas_call(lambda *refs: adapt_kernel(gate_dev, bin_dev, *refs), in_s...  8.49 us
    unnamed x11, local copies, waits for them, and re-layouts  2.86 us
    pallas_call x1, Pallas kernels, swap(): pl.pallas_call(lambda *refs: swap_kernel(gate_dev, rngs, *refs), in_specs...  1.75 us

profile of v4, /device:TPU:0, one launch (start us, length us, event | category | flops | bytes accessed | tf_op | source)
XLA Modules:
  0.0 33.1 jit_solution(13614013111148779618)
XLA Ops:
  0.0 0.0 copy-start.3
  0.0 0.0 copy-start
  0.0 0.9 %copy-done = bf16[32,1024]{1,0:T(8,128)(2,1)S(1)} copy-done((bf16[32,1024]{1,0:T(8,128)(2,1)S(1)}, bf16[32,1024]{1,0:T(8,128)(2,1)}, u32[]{:S(2)}) %copy-start) | copy-done | bytes 65560
  0.9 0.0 copy-start.1
  0.9 0.7 %copy-done.1 = f32[8,512]{1,0:T(8,128)S(1)} copy-done((f32[8,512]{1,0:T(8,128)S(1)}, f32[8,512]{1,0:T(8,128)}, u32[]{:S(2)}) %copy-start.1) | copy-done | bytes 16408
  1.6 0.0 copy-start.2
  1.6 0.7 %copy-done.2 = s32[2,24]{1,0:T(2,128)S(1)} copy-done((s32[2,24]{1,0:T(2,128)S(1)}, s32[2,24]{1,0:T(2,128)}, u32[]{:S(2)}) %copy-start.2) | copy-done | bytes 216
  2.3 0.0 copy-start.4
  2.3 20.0 %shard_map.64.refs_2_ = bf16[4,9,32,128]{3,2,1,0:T(8,128)(2,1)S(1)} custom-call(bf16[32,24,64,128]{3,2,1,0:T(8,128)(2,1)} %bitcast.5, f32[8,512]{1,0:T(8,128)S(1)} %copy-done.1, bf16[32,1024]{1,0:T(8,128)(2,1)S(1)} %copy-done, s32[2,24]{1,0:T(2,128)S(1)} %copy-done.2), custom_call_target="tpu_custom_call" | custom-call | tf_op jit(solution)/shard_map/pallas_call | solution.py:298
  22.2 0.0 copy-done.3
  22.2 0.0 copy-done.4
  22.2 8.5 %shard_map.65.refs_0_ = f32[8,128]{1,0:T(8,128)S(1)} custom-call(f32[2,7]{1,0:T(2,128)S(1)} %copy-done.3, s32[2,4]{1,0:T(2,128)S(1)} %copy-done.4, bf16[4,9,32,128]{3,2,1,0:T(8,128)(2,1)S(1)} %shard_map.64.refs_2_), custom_call_target="tpu_custom_call" | custom-call | tf_op jit(solution)/shard_map/pallas_call | solution.py:542
  30.7 1.7 %shard_map.66 = f32[2,2,4,24]{3,2,1,0:T(4,128)S(1)} custom-call(f32[8,128]{1,0:T(8,128)S(1)} %shard_map.65.refs_0_), custom_call_target="tpu_custom_call" | custom-call | tf_op jit(solution)/shard_map/pallas_call | solution.py:487
  32.5 0.6 %copy.9 = f32[2,2,4,24]{3,2,1,0:T(4,128)} copy(f32[2,2,4,24]{3,2,1,0:T(4,128)S(1)} %shard_map.66) | data formatting | bytes 3072
Async XLA Ops:
  0.0 22.2 %copy-start.3 = (f32[2,7]{1,0:T(2,128)S(1)}, f32[2,7]{1,0:T(2,128)}, u32[]{:S(2)}) copy-start(f32[2,7]{1,0:T(2,128)} %refs_0_.1) | copy-start | bytes 172
  0.0 0.9 %copy-start = (bf16[32,1024]{1,0:T(8,128)(2,1)S(1)}, bf16[32,1024]{1,0:T(8,128)(2,1)}, u32[]{:S(2)}) copy-start(bf16[32,1024]{1,0:T(8,128)(2,1)} %constant.2.clone.table_ref) | copy-start | bytes 196612
  0.9 0.7 %copy-start.1 = (f32[8,512]{1,0:T(8,128)S(1)}, f32[8,512]{1,0:T(8,128)}, u32[]{:S(2)}) copy-start(f32[8,512]{1,0:T(8,128)} %taps_ref.1) | copy-start | bytes 49156
  1.6 0.7 %copy-start.2 = (s32[2,24]{1,0:T(2,128)S(1)}, s32[2,24]{1,0:T(2,128)}, u32[]{:S(2)}) copy-start(s32[2,24]{1,0:T(2,128)} %mask_ref.1) | copy-start | bytes 580
  2.3 20.0 %copy-start.4 = (s32[2,4]{1,0:T(2,128)S(1)}, s32[2,4]{1,0:T(2,128)}, u32[]{:S(2)}) copy-start(s32[2,4]{1,0:T(2,128)} %refs_1_.1) | copy-start | bytes 100

commit v5 on v4

--- a/solution.py
+++ b/solution.py
@@ -317,7 +317,7 @@
             pltpu.SemaphoreType.DMA((rngs,)),
         ],
         compiler_params=pltpu.CompilerParams(
-            collective_id=0, has_side_effects=True, vmem_limit_bytes=53 * 1024 * 1024
+            collective_id=0, has_side_effects=True, vmem_limit_bytes=56 * 1024 * 1024
         ),
     )(view, filter_taps, table, train_mask)
 
@@ -495,7 +495,7 @@
             pltpu.SemaphoreType.DMA,
         ],
         compiler_params=pltpu.CompilerParams(
-            collective_id=1, has_side_effects=True, vmem_limit_bytes=8 * 1024 * 1024
+            collective_id=1, has_side_effects=True, vmem_limit_bytes=56 * 1024 * 1024
         ),
     )(mine)
 
@@ -545,7 +545,7 @@
         out_specs=vmem,
         out_shape=jax.ShapeDtypeStruct((2 * beams, LANES), jnp.float32),
         scratch_shapes=[pltpu.VMEM((dops, gates + 16, LANES), jnp.float32)] * 2,
-        compiler_params=pltpu.CompilerParams(vmem_limit_bytes=32 * 1024 * 1024),
+        compiler_params=pltpu.CompilerParams(vmem_limit_bytes=56 * 1024 * 1024),
     )(range_code, steer, rows)
 
 

time: 33.4 us -> 35.3 us (1.057)
  Pallas kernels: 30.2 us -> 33.7 us
  local copies, waits for them, and re-layouts: 2.86 us -> 1.3 us
    pallas_call x1, Pallas kernels: 8.49 us -> 10.1 us  [adapt(): pl.pallas_call(lambda *refs: adapt_kernel(gate_dev, bin_dev, *refs), in_s...]
    unnamed x11 -> x1, local copies, waits for them, and re-layouts: 2.86 us -> 1.3 us
    pallas_call x1, Pallas kernels: 1.75 us -> 3.01 us  [swap(): pl.pallas_call(lambda *refs: swap_kernel(gate_dev, rngs, *refs), in_specs...]
    pallas_call x1, Pallas kernels: 20 us -> 20.6 us  [gather(): pl.pallas_call(gather_kernel, grid=(gates // block,), in_specs=[pl.BlockS...]
where the time goes in v5:
time: 35.3 us; the launch traced here: 35 us
  Pallas kernels  33.7 us (95%)
  local copies, waits for them, and re-layouts  1.3 us (4%)
    pallas_call x1, Pallas kernels, gather(): pl.pallas_call(gather_kernel, grid=(gates // block,), in_specs=[pl.BlockS...  20.6 us
    pallas_call x1, Pallas kernels, adapt(): pl.pallas_call(lambda *refs: adapt_kernel(gate_dev, bin_dev, *refs), in_s...  10.1 us
    pallas_call x1, Pallas kernels, swap(): pl.pallas_call(lambda *refs: swap_kernel(gate_dev, rngs, *refs), in_specs...  3.01 us
    unnamed x1, local copies, waits for them, and re-layouts  1.3 us

profile of v5, /device:TPU:0, one launch (start us, length us, event | category | flops | bytes accessed | tf_op | source)
XLA Modules:
  0.0 35.0 jit_solution(17462950936884840467)
XLA Ops:
  0.0 20.6 %shard_map.64.refs_2_ = bf16[4,9,32,128]{3,2,1,0:T(8,128)(2,1)} custom-call(bf16[32,24,64,128]{3,2,1,0:T(8,128)(2,1)} %bitcast.5, f32[8,512]{1,0:T(8,128)} %taps_ref.1, bf16[32,1024]{1,0:T(8,128)(2,1)} %constant.2.clone.table_ref, s32[2,24]{1,0:T(2,128)} %mask_ref.1), custom_call_target="tpu_custom_call" | custom-call | tf_op jit(solution)/shard_map/pallas_call | solution.py:298
  20.6 10.1 %shard_map.65.refs_0_ = f32[8,128]{1,0:T(8,128)} custom-call(f32[2,7]{1,0:T(2,128)} %refs_0_.1, s32[2,4]{1,0:T(2,128)} %refs_1_.1, bf16[4,9,32,128]{3,2,1,0:T(8,128)(2,1)} %shard_map.64.refs_2_), custom_call_target="tpu_custom_call" | custom-call | tf_op jit(solution)/shard_map/pallas_call | solution.py:542
  30.7 3.0 %shard_map.66 = f32[2,2,4,24]{3,2,1,0:T(4,128)} custom-call(f32[8,128]{1,0:T(8,128)} %shard_map.65.refs_0_), custom_call_target="tpu_custom_call" | custom-call | tf_op jit(solution)/shard_map/pallas_call | solution.py:487
  33.7 1.3 %copy.9 = f32[2,2,4,24]{3,2,1,0:T(4,128)} copy(f32[2,2,4,24]{3,2,1,0:T(4,128)} %shard_map.66) | data formatting | bytes 3072
